TPU v7x, 256 devices: a whole 4x4x8 slice. The times are simulated.
256 devices in a mesh: dp: 8 (over x, core), vocab: 32 (over z, y).
Axes of the slice: x: 4, y: 4, z: 8, core: 2. Of those that a mesh axis runs over, the one named last changes fastest.
Arguments:
- hidden: bfloat16 [1024, 3584], P('dp'), may hold values from -64 to 64
- head_weight: bfloat16 [3584, 131072], P('dp', 'vocab'), may hold values from -0.15039062 to 0.15039062
- teacher_logits: float32 [1024, 131072], P('dp', 'vocab'), may hold values from -32 to 480
Outputs:
- divergence: float32 [1024], P('dp')
- hidden_gradient: bfloat16 [1024, 3584], P('vocab', 'dp')
- head_gradient: bfloat16 [3584, 131072], P('dp', 'vocab')
All inputs are finite; a program needn't handle non-finite values.
Results may differ from a plain program's by a relative error of at most 0.0043.
Values may be sent and summed in bfloat16 or wider, within the bound.
A program may use at most 128 MiB of HBM per device.

v0:
```python
import jax
import jax.numpy as jnp
from jax import lax
from jax.sharding import PartitionSpec as P

loss_scale = 256.0


def local(hidden, head_weight, teacher_logits):
    columns = lax.all_to_all(hidden, "dp", split_axis=1, concat_axis=0, tiled=True)
    student = jnp.dot(
        hidden,
        lax.all_gather(head_weight, "dp", axis=0, tiled=True),
        preferred_element_type=jnp.float32,
    )
    local_student_max = jnp.max(student, axis=1)
    local_teacher_max = jnp.max(teacher_logits, axis=1)
    student_max, teacher_max = lax.pmax((local_student_max, local_teacher_max), "vocab")
    student_exp = jnp.exp(student - student_max[:, None])
    teacher_exp = jnp.exp(teacher_logits - teacher_max[:, None])
    student_sum, teacher_sum, cross_sum = lax.psum(
        (
            jnp.sum(student_exp, axis=1),
            jnp.sum(teacher_exp, axis=1),
            jnp.sum(teacher_exp * (teacher_logits - student), axis=1),
        ),
        "vocab",
    )
    divergence = (
        cross_sum / teacher_sum
        - teacher_max
        - jnp.log(teacher_sum)
        + student_max
        + jnp.log(student_sum)
    )
    grad_logits = (
        loss_scale * (student_exp / student_sum[:, None] - teacher_exp / teacher_sum[:, None])
    ).astype(jnp.bfloat16)
    all_grads = lax.all_gather(grad_logits, "dp", axis=0, tiled=True)
    hidden_gradient = lax.psum_scatter(
        lax.dot_general(
            all_grads, head_weight, (((1,), (1,)), ((), ())), preferred_element_type=jnp.float32
        ),
        "vocab",
        scatter_dimension=0,
        tiled=True,
    ).astype(jnp.bfloat16)
    head_gradient = lax.dot_general(
        columns, all_grads, (((0,), (0,)), ((), ())), preferred_element_type=jnp.float32
    ).astype(jnp.bfloat16)
    return (divergence, hidden_gradient, head_gradient)


def solution(mesh):
    return jax.shard_map(
        local,
        mesh=mesh,
        in_specs=(P("dp", None), P("dp", "vocab"), P("dp", "vocab")),
        out_specs=(P("dp"), P("vocab", "dp"), P("dp", "vocab")),
        check_vma=False,
    )
```

profile of v0, /device:TPU:24, one launch (start us, length us, event | category | flops | bytes accessed | tf_op | source)
XLA Modules:
  0.0 599.2 jit_solution(17285911199094920289)
XLA Ops:
  7.2 0.0 copy-start
  7.2 0.0 copy-start.1
  7.2 0.0 all-gather.3.cloned.1.call-start
  7.2 0.7 all-gather.3.cloned.1.call-update
  7.9 0.0 all-gather.5.cloned.1.call-start
  8.0 0.8 copy-done
  8.8 0.2 reduce_max.18
  8.9 144.3 %all-gather.3.cloned.1.call-done = bf16[3584,4096]{1,0:T(8,128)(2,1)} async-done(((bf16[448,4096]{1,0:T(8,128)(2,1)}), bf16[3584,4096]{1,0:T(8,128)(2,1)}) %all-gather.3.cloned.1.call-update) | async-done | bytes 29360144 | tf_op jit(solution)/shard_map/all_gather | solution.py:13
  153.2 0.0 copy-done.1
  153.2 11.5 %fusion.5 = (f32[128]{0:T(128)S(1)}, f32[128,4096]{1,0:T(8,128)S(1)}) fusion(bf16[128,3584]{1,0:T(8,128)(2,1)S(1)} %copy-done.1, bf16[3584,4096]{1,0:T(8,128)(2,1)} %all-gather.3.cloned.1.call-done), kind=kOutput, calls=%fused_computation.11 | convolution fusion | flops 3758620672 | bytes 32375296 | tf_op jit(solution)/shard_map/dot_general | solution.py:11
  164.7 67.2 %all-reduce.1 = (f32[128]{0:T(128)S(1)}, f32[128]{0:T(128)S(1)}) all-reduce(f32[128]{0:T(128)S(1)} %reduce_max.18, f32[128]{0:T(128)S(1)} %get-tuple-element.11), channel_id=1, replica_groups=mesh['dp'=8,'vocab'=32] {'vocab'}, use_global_device_ids=true, to_apply=%region_1.0 | all-reduce | flops 256 | bytes 2048 | tf_op jit(solution)/shard_map/pmax | solution.py:18
  231.9 2.5 multiply_reduce_fusion
  234.4 74.2 %all-reduce = (f32[128]{0:T(128)S(1)}, f32[128]{0:T(128)S(1)}, f32[128]{0:T(128)S(1)}) all-reduce(f32[128]{0:T(128)S(1)} %get-tuple-element.5, f32[128]{0:T(128)S(1)} %get-tuple-element.4, f32[128]{0:T(128)S(1)} %get-tuple-element.3), channel_id=1, replica_groups=mesh['dp'=8,'vocab'=32] {'vocab'}, use_global_device_ids=true, to_apply=%region_9.0 | all-reduce | flops 384 | bytes 3072 | tf_op jit(solution)/shard_map/psum | solution.py:21
  308.6 3.4 multiply_convert_fusion
  312.0 0.0 all-gather.5.cloned.1.call-update
  312.0 0.0 reduce-scatter.2.cloned.1.call-start
  312.1 52.9 %all-gather.5.cloned.1.call-done = bf16[1024,4096]{1,0:T(8,128)(2,1)} async-done(((bf16[128,4096]{1,0:T(8,128)(2,1)}), bf16[1024,4096]{1,0:T(8,128)(2,1)}) %all-gather.5.cloned.1.call-update) | async-done | bytes 8388624 | tf_op jit(solution)/shard_map/all_gather | solution.py:39
  365.0 10.3 %fusion.6 = f32[1024,448]{1,0:T(8,128)} fusion(bf16[1024,4096]{1,0:T(8,128)(2,1)} %all-gather.5.cloned.1.call-done, bf16[448,4096]{1,0:T(8,128)(2,1)} %param.4), kind=kOutput, calls=%fused_computation.12 | convolution fusion | flops 3758096384 | bytes 13893632 | tf_op jit(solution)/shard_map/dot_general | solution.py:41
  375.3 0.0 reduce-scatter.2.cloned.1.call-update
  375.4 1.3 copy.6
  376.6 3.6 all-to-all-start
  380.2 0.5 log_add_fusion
  380.7 14.0 %all-to-all-done = bf16[128,8,448]{0,2,1:T(8,128)(2,1)S(1)} async-done(((bf16[128,8,448]{0,2,1:T(8,128)(2,1)}), bf16[128,8,448]{0,2,1:T(8,128)(2,1)S(1)}, u32[]{:S(2)}, u32[]{:S(2)}) %all-to-all-start) | async-done | bytes 917536 | tf_op jit(solution)/shard_map/all_to_all | solution.py:10
  394.7 8.9 %fusion = bf16[448,4096]{1,0:T(8,128)(2,1)} fusion(bf16[1024,4096]{1,0:T(8,128)(2,1)} %all-gather.5.cloned.1.call-done, bf16[128,8,448]{0,2,1:T(8,128)(2,1)S(1)} %all-to-all-done), kind=kOutput, calls=%fused_computation.1 | convolution fusion | flops 3759931392 | bytes 12976128 | tf_op jit(solution)/shard_map/dot_general | solution.py:48
  403.6 187.6 %reduce-scatter.2.cloned.1.call-done = f32[32,448]{1,0:T(8,128)} async-done(((f32[1024,448]{1,0:T(8,128)}), f32[32,448]{1,0:T(8,128)}) %reduce-scatter.2.cloned.1.call-update) | async-done | bytes 57360 | tf_op jit(solution)/shard_map/reduce_scatter | solution.py:40
  591.2 1.5 convert_element_type.13
Async XLA Ops:
  7.2 1.6 copy-start
  7.2 146.1 %copy-start.1 = (bf16[128,3584]{1,0:T(8,128)(2,1)S(1)}, bf16[128,3584]{1,0:T(8,128)(2,1)}, u32[]{:S(2)}) copy-start(bf16[128,3584]{1,0:T(8,128)(2,1)} %param.3) | copy-start | bytes 2752516
  7.2 146.0 %all-gather.3.cloned.1.call-start = ((), (), s32[]{:S(2)}) async-start(), calls=%async_computation.2 | async-start | bytes 33030144 | tf_op jit(solution)/shard_map/all_gather | solution.py:13
  7.9 357.1 %all-gather.5.cloned.1.call-start = ((), (), s32[]{:S(2)}) async-start(), calls=%async_computation.3 | async-start | bytes 9437184 | tf_op jit(solution)/shard_map/all_gather | solution.py:39
  312.0 279.1 %reduce-scatter.2.cloned.1.call-start = ((), (), s32[]{:S(2)}) async-start(), calls=%async_computation.4 | async-start | bytes 2162688 | tf_op jit(solution)/shard_map/reduce_scatter | solution.py:40
  376.6 18.0 %all-to-all-start = ((bf16[128,8,448]{0,2,1:T(8,128)(2,1)}), bf16[128,8,448]{0,2,1:T(8,128)(2,1)S(1)}, u32[]{:S(2)}, u32[]{:S(2)}) async-start(bf16[128,8,448]{0,2,1:T(8,128)(2,1)} %bitcast), calls=%async_computation.1 | async-start | bytes 1835008 | tf_op jit(solution)/shard_map/all_to_all | solution.py:10
Sparse Core Ops, SparseCore 0:
  9.9 143.3 all-gather.2
  312.1 52.8 all-gather.4
  375.5 215.6 reduce-scatter.1
where the time goes:
time: 601 us; the launch traced here: 599 us
  waiting for transfers between devices  399 us (66%)
  blocking collectives  141 us (23%)
  matrix products  30.7 us (5%)
  between operations  13.8 us (2%)
  other arithmetic  8.1 us (1%)
    reduce_scatter x1, waiting for transfers between devices, local(): lax.psum_scatter(lax.dot_general(all_grads, head_weight, (((1,), (1,)), (...  188 us
    all_gather x1, waiting for transfers between devices, local(): lax.all_gather(head_weight, 'dp', axis=0, tiled=True)  144 us
    psum x1, blocking collectives, local(): lax.psum((jnp.sum(student_exp, axis=1), jnp.sum(teacher_exp, axis=1), jnp...  74.2 us
    pmax x1, blocking collectives, local(): lax.pmax((local_student_max, local_teacher_max), 'vocab')  67.2 us
    all_gather x1, waiting for transfers between devices, local(): all_grads = lax.all_gather(grad_logits, 'dp', axis=0, tiled=True)  52.9 us
    all_to_all x1, waiting for transfers between devices, local(): lax.all_to_all(hidden, 'dp', split_axis=1, concat_axis=0, tiled=True)  14 us
  transfers between devices with their start and end apart: 4, of which 4 were waited for; matrix products, arithmetic and copies ran while one was open for 2% of the time, Pallas kernels for 0%

commit v1 on v0

v1 whole, which is shorter than its diff:
```python
import jax
import jax.numpy as jnp
from jax import lax
from jax.experimental import pallas as pl
from jax.experimental.pallas import tpu as pltpu
from jax.sharding import PartitionSpec as P

MESH = pl.DeviceIdType.MESH
F32, BF16 = jnp.float32, jnp.bfloat16
loss_scale = 256.0
LOW = -3.0e38

D, ROWS = 3584, 1024
NX, NY, NZ = 4, 4, 8
BLK = 128
SUB = BLK // NY
WID = D // 8
CHIP = 2 * WID
COLS = 4096
PART = COLS // NX
HSH = D // NY


def groups(value):
    return [value[:, 128 * g : 128 * g + 128] for g in range(value.shape[1] // 128)]


def fold(parts, op):
    while len(parts) > 1:
        parts = [op(parts[i], parts[i + 1]) for i in range(0, len(parts), 2)]
    return parts[0]


def row_max(part):
    return jnp.max(part.T, axis=0, keepdims=True)


def row_sum(part):
    return jnp.sum(part.T, axis=0, keepdims=True)


def kernel(
    h_ref, w_ref, t_ref,
    div_ref, hg_ref, dw_ref,
    hc, wc, tc, student, town, wown, wt, hx, ht, gbuf, acc, stage,
    hgp, hgy, hgz, sx, sy, sz, col, cross, cx, cy, cz,
    lsem, osem, hxs, hxr, hys, hyr, wxs, wxr, wcs, wcr, ts, tr, hcs, hcr,
    sxs, sxr, sys_, syr, szs, szr, gas, gar, gfs, gfr, gcs, gcr,
    hgys, hgyr, hgzs, hgzr, cxs, cxr, cys, cyr, czs, czr,
):
    dp, v = lax.axis_index("dp"), lax.axis_index("vocab")
    x, c = dp // 2, dp % 2
    z, y = v // NY, v % NY

    def at_x(o):
        return (lax.rem(x + o, NX) * 2 + c, v)

    def at_y(o):
        return (dp, z * NY + lax.rem(y + o, NY))

    def at_z(o):
        return (dp, lax.rem(z + o, NZ) * NY + y)

    other = (x * 2 + 1 - c, v)

    def remote(src, dst, ss, rs, device):
        return pltpu.make_async_remote_copy(
            src_ref=src, dst_ref=dst, send_sem=ss, recv_sem=rs, device_id=device, device_id_type=MESH
        )

    barrier = pltpu.get_barrier_semaphore()
    partners = [at_x(o) for o in range(1, NX)] + [other]
    partners += [at_y(o) for o in range(1, NY)] + [at_z(o) for o in range(1, NZ)]
    for p in partners:
        pl.semaphore_signal(barrier, inc=1, device_id=p, device_id_type=MESH)

    def cols_of(i):
        return pl.ds(pl.multiple_of(i * PART, PART), PART)

    def rows_of(i):
        return pl.ds(pl.multiple_of(i * BLK, BLK), BLK)

    def wrows(i, j):
        return pl.ds(pl.multiple_of(i * CHIP + j * WID, 64), WID)

    own_w = pltpu.make_async_copy(w_ref.at[:, cols_of(x)], wc.at[wrows(x, c)], lsem.at[0])
    share = pl.ds(pl.multiple_of(y * HSH, HSH), HSH)
    own_h = pltpu.make_async_copy(h_ref.at[:, share], hc.at[rows_of(x), share], lsem.at[1])
    own_t = pltpu.make_async_copy(t_ref.at[:, cols_of(x)], tc.at[x], lsem.at[2])
    all_t = pltpu.make_async_copy(t_ref, town, lsem.at[3])
    all_w = pltpu.make_async_copy(w_ref, wown, lsem.at[4])
    for cp in (own_h, all_t, all_w, own_w, own_t):
        cp.start()
    pl.semaphore_wait(barrier, len(partners))

    h_x = [
        remote(h_ref.at[:, share], hc.at[rows_of(x), share], hxs.at[o - 1], hxr.at[o - 1], at_x(o))
        for o in range(1, NX)
    ]
    w_x = [
        remote(
            w_ref.at[:, cols_of(lax.rem(x + o, NX))], wc.at[wrows(x, c)], wxs.at[o - 1], wxr.at[o - 1], at_x(o)
        )
        for o in range(1, NX)
    ]
    t_x = [
        remote(t_ref.at[:, cols_of(lax.rem(x + o, NX))], tc.at[x], ts.at[o - 1], tr.at[o - 1], at_x(o))
        for o in range(1, NX)
    ]

    def w_core(o):
        rows = wrows(lax.rem(x + NX - o, NX), c)
        src = w_ref.at[:, cols_of(x)] if o == 0 else wc.at[rows]
        return remote(src, wc.at[rows], wcs.at[o], wcr.at[o], other)

    w_c = [w_core(o) for o in range(NX)]
    for cp in h_x + w_x:
        cp.start()
    w_c[0].start()

    own_h.wait()
    for cp in h_x:
        cp.wait_recv()
    h_y = [
        remote(hc.at[:, share], hc.at[:, share], hys.at[o - 1], hyr.at[o - 1], at_y(o)) for o in range(1, NY)
    ]
    for cp in h_y:
        cp.start()

    for b in range(NX):
        sx[x, b] = jnp.where(lax.broadcasted_iota(jnp.int32, (8, BLK), 0) % 2 == 0, LOW, 0.0)
    all_t.wait()
    part = fold([town[:, 128 * g : 128 * g + 128] for g in range(COLS // 128)], jnp.maximum)
    top = jnp.max(part, axis=1, keepdims=True)
    total = fold([jnp.exp(town[:, 128 * g : 128 * g + 128] - top) for g in range(COLS // 128)], jnp.add)
    sx[x, x, 2:3, :] = row_max(part)
    sx[x, x, 3:4, :] = row_sum(total)

    all_w.wait()

    def turn(i, carry):
        cols = pl.ds(pl.multiple_of(i * 512, 512), 512)
        wt[cols, :] = wown[:, cols].T
        return carry

    lax.fori_loop(0, COLS // 512, turn, 0)

    for o in (1, 3, 2):
        w_x[o - 1].wait_recv()
        w_c[o].start()
    for cp in w_x:
        cp.wait_send()
    for cp in t_x:
        cp.start()
    for cp in h_y:
        cp.wait_recv()

    mine = pl.ds(pl.multiple_of(x * CHIP, CHIP), CHIP)
    h_c = remote(hc.at[:, mine], hx.at[c], hcs.at[0], hcr.at[0], other)
    h_c.start()
    keep = pltpu.make_async_copy(hc.at[:, mine], hx.at[c], lsem.at[5])
    keep.start()
    own_w.wait()
    for cp in w_c:
        cp.wait_recv()

    def score(i, carry):
        cols = pl.ds(pl.multiple_of(i * 256, 256), 256)
        tile = jnp.dot(hc[...], wc[:, cols], preferred_element_type=F32)
        student[:, :, cols] = tile.reshape(NX, BLK, 256)
        return carry

    lax.fori_loop(0, PART // 256, score, 0)

    def local_stats(b, carry):
        parts = groups(student[b])
        part = fold(parts, jnp.maximum)
        top = jnp.max(part, axis=1, keepdims=True)
        total = fold([jnp.exp(p - top) for p in parts], jnp.add)
        sx[x, b, 0:1, :] = row_max(part)
        sx[x, b, 1:2, :] = row_sum(total)
        return carry

    lax.fori_loop(0, NX, local_stats, 0)

    def reduce_stats(slots, count, target):
        for b in range(NX):
            m_s = fold([slots[i, b, 0:1, :] for i in range(count)], jnp.maximum)
            m_t = fold([slots[i, b, 2:3, :] for i in range(count)], jnp.maximum)
            l_s = fold([slots[i, b, 1:2, :] * jnp.exp(slots[i, b, 0:1, :] - m_s) for i in range(count)], jnp.add)
            l_t = fold([slots[i, b, 3:4, :] * jnp.exp(slots[i, b, 2:3, :] - m_t) for i in range(count)], jnp.add)
            target(b, m_s, l_s, m_t, l_t)

    def into(slots, me):
        def put(b, *values):
            for r, value in enumerate(values):
                slots[me, b, r : r + 1, :] = value

        return put

    s_x = [remote(sx.at[x], sx.at[x], sxs.at[o - 1], sxr.at[o - 1], at_x(o)) for o in range(1, NX)]
    s_y = [remote(sy.at[y], sy.at[y], sys_.at[o - 1], syr.at[o - 1], at_y(o)) for o in range(1, NY)]
    s_z = [remote(sz.at[z], sz.at[z], szs.at[o - 1], szr.at[o - 1], at_z(o)) for o in range(1, NZ)]
    for cp in s_x:
        cp.start()
    keep.wait()
    h_c.wait_recv()

    def turn_h(k, carry):
        rows = [
            hx[j, pl.ds(pl.multiple_of(BLK * b + SUB * k, SUB), SUB), :] for j in range(2) for b in range(NX)
        ]
        block = jnp.concatenate(rows, axis=0).astype(F32)
        block = pltpu.roll(block, lax.rem(c * WID, CHIP), 1)[:, :512]
        ht[k] = block.T[:WID].astype(BF16)
        return carry

    lax.fori_loop(0, NY, turn_h, 0)
    for cp in s_x:
        cp.wait_recv()
    reduce_stats(sx, NX, into(sy, y))
    for cp in s_y:
        cp.start()
    for cp in s_y:
        cp.wait_recv()
    reduce_stats(sy, NY, into(sz, z))
    for cp in s_z:
        cp.start()
    for cp in s_z:
        cp.wait_recv()

    def columns(b, m_s, l_s, m_t, l_t):
        for r, value in enumerate((m_s, loss_scale / l_s, m_t, loss_scale / l_t)):
            col[r, b] = jnp.broadcast_to(value, (BLK, BLK)).T
        sx[0, b, 4:5, :] = m_s + jnp.log(l_s) - m_t - jnp.log(l_t)
        sx[0, b, 5:6, :] = l_t

    for cp in s_x:
        cp.wait_send()
    reduce_stats(sz, NZ, columns)

    own_t.wait()
    for cp in t_x:
        cp.wait_recv()

    def half(s, owner, first):
        return gbuf.at[s, pl.ds(pl.multiple_of(c * BLK + first, 64), BLK // 2), cols_of(owner)]

    def whole(s, owner):
        return gbuf.at[s, pl.ds(pl.multiple_of(c * BLK, BLK), BLK), cols_of(owner)]

    left, right, far = lax.rem(x + 3, NX), lax.rem(x + 1, NX), lax.rem(x + 2, NX)
    owners = [x, left, far, right]
    g_a, g_f, g_c = [], [], []
    for s in range(NY):
        g_a.append(
            [remote(whole(s, x), whole(s, x), gas.at[s, i], gar.at[s, i], at_x(o)) for i, o in enumerate((1, 3))]
        )
        g_f.append(
            [
                remote(half(s, left, 0), half(s, left, 0), gfs.at[s, 0], gfr.at[s, 0], at_x(1)),
                remote(half(s, right, 64), half(s, right, 64), gfs.at[s, 1], gfr.at[s, 1], at_x(3)),
            ]
        )
        g_c.append(
            [remote(whole(s, q), whole(s, q), gcs.at[s, o], gcr.at[s, o], other) for o, q in enumerate(owners)]
        )

    for s in range(NY):
        k = lax.rem(y + 1 + s, NY)
        rows = pl.ds(pl.multiple_of(k * SUB, SUB), SUB)

        def grad(b, carry):
            m_s, a_s, m_t, a_t = [col[r, b, rows, :] for r in range(4)]
            out = pl.ds(pl.multiple_of(c * BLK + b * SUB, SUB), SUB)
            total = jnp.zeros((SUB, 128), F32)
            tiles = []
            for g in range(PART // 128):
                st = student[b, rows, 128 * g : 128 * g + 128]
                te = tc[b, rows, 128 * g : 128 * g + 128]
                e_t = jnp.exp(te - m_t)
                total += e_t * (te - st)
                tiles.append((jnp.exp(st - m_s) * a_s - e_t * a_t).astype(BF16))
            gbuf[s, out, cols_of(x)] = jnp.concatenate(tiles, axis=1)
            cross[b, rows, :] = total
            return carry

        lax.fori_loop(0, NX, grad, 0)
        for cp in g_a[s]:
            cp.start()
        g_c[s][0].start()

    for b in range(NX):
        cx[x, b] = jnp.broadcast_to(row_sum(cross[b]), (8, BLK))
    c_x = [
        remote(
            cx.at[x, lax.rem(x + o, NX)], cx.at[x, lax.rem(x + o, NX)], cxs.at[o - 1], cxr.at[o - 1], at_x(o)
        )
        for o in range(1, NX)
    ]
    c_y = [remote(cy.at[y], cy.at[y], cys.at[o - 1], cyr.at[o - 1], at_y(o)) for o in range(1, NY)]
    c_z = [remote(cz.at[z], cz.at[z], czs.at[o - 1], czr.at[o - 1], at_z(o)) for o in range(1, NZ)]
    for cp in c_x:
        cp.start()

    h_to_y = [
        remote(hgp.at[o - 1], hgy.at[o - 1], hgys.at[o - 1], hgyr.at[o - 1], at_y(o)) for o in range(1, NY)
    ]

    def z_rows(o):
        zz = lax.rem(z + o, NZ)
        return pl.ds(pl.multiple_of((zz % 2) * BLK + (zz // 2) * SUB, SUB), SUB)

    h_to_z = [
        remote(hgp.at[3, z_rows(o)], hgz.at[o - 1], hgzs.at[o - 1], hgzr.at[o - 1], at_z(o))
        for o in range(1, NZ)
    ]
    d_out = []
    for s in range(NY):
        k = lax.rem(y + 1 + s, NY)
        g_a[s][0].wait_recv()
        g_f[s][0].start()
        g_c[s][1].start()
        g_a[s][1].wait_recv()
        g_f[s][1].start()
        g_c[s][3].start()
        for cp in g_f[s]:
            cp.wait_recv()
        g_c[s][2].start()
        if s == 1:
            for cp in c_x:
                cp.wait_recv()
            cy[y] = cx[0, x] + cx[1, x] + cx[2, x] + cx[3, x]
            for cp in c_y:
                cp.start()
        if s == 2:
            for cp in c_y:
                cp.wait_recv()
            cz[z] = cy[0] + cy[1] + cy[2] + cy[3]
            for cp in c_z:
                cp.start()
        for cp in g_c[s]:
            cp.wait_recv()
        product = jnp.dot(gbuf[s], wt[...], preferred_element_type=F32)
        if s < 3:
            hgp[s] = product
            h_to_y[s].start()
        else:
            for cp in h_to_y:
                cp.wait_recv()
            hgp[3] = product + hgy[0] + hgy[1] + hgy[2]
            for cp in h_to_z:
                cp.start()

        def head(i, carry):
            cols = pl.ds(pl.multiple_of(i * 512, 512), 512)
            tile = jnp.dot(ht[k], gbuf[s, :, cols], preferred_element_type=F32)
            if s == 0:
                acc[:, cols] = tile
            elif s < 3:
                acc[:, cols] += tile
            else:
                stage[:, cols] = (acc[:, cols] + tile).astype(BF16)
            return carry

        if s < 3:
            lax.fori_loop(0, COLS // 512, head, 0)
        else:
            for i in range(NX):
                lax.fori_loop(2 * i, 2 * i + 2, head, 0)
                cols = pl.ds(i * PART, PART)
                d_out.append(pltpu.make_async_copy(stage.at[:, cols], dw_ref.at[:, cols], osem.at[i]))
                d_out[-1].start()

    for cp in c_z:
        cp.wait_recv()
    crossed = fold([cz[i, 0:1, :] for i in range(NZ)], jnp.add)
    div_ref[...] = crossed / sx[0, x, 5:6, :] + sx[0, x, 4:5, :]

    for cp in h_to_z:
        cp.wait_recv()
    total = hgp[3, z_rows(0), :]
    for i in range(NZ - 1):
        total = total + hgz[i]
    hg_ref[...] = total.astype(BF16)

    for cp in d_out:
        cp.wait()
    sent = h_x + w_c + h_y + t_x + [h_c] + s_y + s_z + c_x + c_y + c_z + h_to_y + h_to_z
    for cp in sent + sum(g_a, []) + sum(g_f, []) + sum(g_c, []):
        cp.wait_send()


def local(hidden, head_weight, teacher_logits):
    dma = pltpu.SemaphoreType.DMA
    vmem = pltpu.VMEM
    scratch = [
        vmem((NX * BLK, D), BF16),
        vmem((D, PART), BF16),
        vmem((NX, BLK, PART), F32),
        vmem((NX, BLK, PART), F32),
        vmem((BLK, COLS), F32),
        vmem((WID, COLS), BF16),
        vmem((COLS, WID), BF16),
        vmem((2, NX * BLK, CHIP), BF16),
        vmem((NY, WID, 2 * BLK), BF16),
        vmem((NY, 2 * BLK, COLS), BF16),
        vmem((WID, COLS), F32),
        vmem((WID, COLS), BF16),
        vmem((NY, 2 * BLK, WID), F32),
        vmem((NY - 1, 2 * BLK, WID), F32),
        vmem((NZ - 1, SUB, WID), F32),
        vmem((NX, NX, 8, BLK), F32),
        vmem((NY, NX, 8, BLK), F32),
        vmem((NZ, NX, 8, BLK), F32),
        vmem((4, NX, BLK, BLK), F32),
        vmem((NX, BLK, BLK), F32),
        vmem((NX, NX, 8, BLK), F32),
        vmem((NY, 8, BLK), F32),
        vmem((NZ, 8, BLK), F32),
    ]
    counts = [(3,), (3,), (3,), (4,), (3,), (1,), (3,), (3,), (7,), (4, 2), (4, 2), (4, 4), (3,), (7,), (3,), (3,), (7,)]
    sems = [dma((6,)), dma((4,))]
    for n in counts:
        sems += [dma(n), dma(n)]
    div, hg, dw = pl.pallas_call(
        kernel,
        name="distill",
        out_shape=(
            jax.ShapeDtypeStruct((1, BLK), F32),
            jax.ShapeDtypeStruct((SUB, WID), BF16),
            jax.ShapeDtypeStruct((WID, COLS), BF16),
        ),
        in_specs=[pl.BlockSpec(memory_space=pl.ANY)] * 3,
        out_specs=(
            pl.BlockSpec(memory_space=pltpu.VMEM),
            pl.BlockSpec(memory_space=pltpu.VMEM),
            pl.BlockSpec(memory_space=pl.ANY),
        ),
        scratch_shapes=scratch + sems,
        compiler_params=pltpu.CompilerParams(
            collective_id=0, has_side_effects=True, vmem_limit_bytes=60 * 1024 * 1024
        ),
    )(hidden, head_weight, teacher_logits)
    return div.reshape(BLK), hg, dw


def solution(mesh):
    return jax.shard_map(
        local,
        mesh=mesh,
        in_specs=(P("dp", None), P("dp", "vocab"), P("dp", "vocab")),
        out_specs=(P("dp"), P("vocab", "dp"), P("dp", "vocab")),
        check_vma=False,
    )
```

time: 601 us -> 183 us (0.30)
  waiting for transfers between devices: 399 us -> 0 us
  Pallas kernels: 0 us -> 173 us
  blocking collectives: 141 us -> 0 us
  matrix products: 30.7 us -> 0 us
  between operations: 13.8 us -> 0.64 us
  other arithmetic: 8.1 us -> 0 us
    all_gather x2 -> x0, waiting for transfers between devices: 197 us -> none  [the longest x1 144 us: local(): lax.all_gather(head_weight, 'dp', axis=0, tiled=True)]
    reduce_scatter x1 -> x0, waiting for transfers between devices: 188 us -> none  [local(): lax.psum_scatter(lax.dot_general(all_grads, head_weight, (((1,), (1,)), (...]
    pallas_call x0 -> x1, Pallas kernels: none -> 173 us  [local(): pl.pallas_call(kernel, name='distill', out_shape=(jax.ShapeDtypeStruct((1...]
    psum x1 -> x0, blocking collectives: 74.2 us -> none  [local(): lax.psum((jnp.sum(student_exp, axis=1), jnp.sum(teacher_exp, axis=1), jnp...]
    pmax x1 -> x0, blocking collectives: 67.2 us -> none  [local(): lax.pmax((local_student_max, local_teacher_max), 'vocab')]
    dot_general x3 -> x0, matrix products: 30.7 us -> none  [the longest x1 11.5 us: local(): jnp.dot(hidden, lax.all_gather(head_weight, 'dp', axis=0, tiled=True), pr...]
    all_to_all x1 -> x0, waiting for transfers between devices: 14 us -> none  [local(): lax.all_to_all(hidden, 'dp', split_axis=1, concat_axis=0, tiled=True)]
  transfers between devices with their start and end apart: 4 -> 0, of which waited for: 4 -> 0; matrix products, arithmetic and copies ran while one was open for 2% -> 0% of each run, Pallas kernels for 0% -> 0%
where the time goes in v1:
time: 183 us; the launch traced here: 180 us
  Pallas kernels  173 us (95%)
  local copies, waits for them, and re-layouts  6.79 us (4%)
    pallas_call x1, Pallas kernels, local(): pl.pallas_call(kernel, name='distill', out_shape=(jax.ShapeDtypeStruct((1...  173 us
    unnamed x3, local copies, waits for them, and re-layouts  6.79 us

profile of v1, /device:TPU:24, one launch (start us, length us, event | category | flops | bytes accessed | tf_op | source)
XLA Modules:
  0.0 180.2 jit_solution(15508137446404863369)
XLA Ops:
  0.6 172.8 %distill.1 = (f32[1,128]{1,0:T(1,128)}, bf16[32,448]{1,0:T(8,128)(2,1)}, bf16[448,4096]{1,0:T(8,128)(2,1)}) custom-call(bf16[128,3584]{1,0:T(8,128)(2,1)} %h_ref.1, bf16[448,4096]{1,0:T(8,128)(2,1)} %w_ref.1, f32[128,4096]{1,0:T(8,128)} %t_ref.1), custom_call_target="tpu_custom_call" | custom-call | tf_op jit(solution)/shard_map/distill/pallas_call | solution.py:426
  173.4 1.1 copy.9
  174.5 1.4 copy.10
  175.9 4.3 %copy.11 = bf16[448,4096]{1,0:T(8,128)(2,1)} copy(bf16[448,4096]{1,0:T(8,128)(2,1)} %get-tuple-element.14) | data formatting | bytes 7340032

commit v2 on v1

v2 whole, which is shorter than its diff:
```python
import jax
import jax.numpy as jnp
from jax import lax
from jax.experimental import pallas as pl
from jax.experimental.pallas import tpu as pltpu
from jax.sharding import PartitionSpec as P

MESH = pl.DeviceIdType.MESH
F32, BF16 = jnp.float32, jnp.bfloat16
loss_scale = 256.0
LOW = -3.0e38

D, ROWS = 3584, 1024
NX, NY, NZ = 4, 4, 8
BLK = 128
SUB = BLK // NY
WID = D // 8
CHIP = 2 * WID
COLS = 4096
PART = COLS // NX
HSH = D // NY
HALF = BLK // 2


STEPS = ((1, 0, 32), (2, 0, 32), (3, 0, 32), (0, 0, 16), (0, 16, 16))
BIG = 2 * NX * SUB
FIRST = (0, BIG, 2 * BIG, 3 * BIG, 3 * BIG + BIG // 2)


def groups(value):
    return [value[:, 128 * g : 128 * g + 128] for g in range(value.shape[1] // 128)]


def fold(parts, op):
    while len(parts) > 1:
        parts = [op(parts[i], parts[i + 1]) for i in range(0, len(parts), 2)]
    return parts[0]


def row_max(part):
    return jnp.max(part.T, axis=0, keepdims=True)


def row_sum(part):
    return jnp.sum(part.T, axis=0, keepdims=True)


def kernel(
    h_ref, w_ref, t_ref,
    div_ref, hg_ref, dw_ref,
    hc, wc, tc, student, town, wown, wt, hx, ht, gbuf, acc,
    hgp, hgy, hgz, sx, sy, sz, last, col, cross, cx, cy, cz,
    lsem, hxs, hxr, hzs, hzr, hys, hyr, wxs, wxr, wcs, wcr, ts, tr, hcs, hcr,
    sxs, sxr, sys_, syr, szs, szr, gas, gar, gfs, gfr, gcs, gcr,
    hgys, hgyr, hgzs, hgzr, cxs, cxr, cys, cyr, czs, czr,
):
    dp, v = lax.axis_index("dp"), lax.axis_index("vocab")
    x, c = dp // 2, dp % 2
    z, y = v // NY, v % NY

    def at_x(o):
        return (lax.rem(x + o, NX) * 2 + c, v)

    def at_y(o):
        return (dp, z * NY + lax.rem(y + o, NY))

    def at_z(o):
        return (dp, lax.rem(z + o, NZ) * NY + y)

    other = (x * 2 + 1 - c, v)
    beside = (dp, (z + 1 - 2 * (z % 2)) * NY + y)

    def remote(src, dst, ss, rs, device):
        return pltpu.make_async_remote_copy(
            src_ref=src, dst_ref=dst, send_sem=ss, recv_sem=rs, device_id=device, device_id_type=MESH
        )

    barrier = pltpu.get_barrier_semaphore()
    partners = [at_x(o) for o in range(1, NX)] + [other]
    partners += [at_y(o) for o in range(1, NY)] + [at_z(o) for o in range(1, NZ)]
    for p in partners:
        pl.semaphore_signal(barrier, inc=1, device_id=p, device_id_type=MESH)

    def cols_of(i):
        return pl.ds(pl.multiple_of(i * PART, PART), PART)

    def wrows(i, j):
        return pl.ds(pl.multiple_of(i * CHIP + j * WID, 64), WID)

    own_w = pltpu.make_async_copy(w_ref.at[:, cols_of(x)], wc.at[wrows(x, c)], lsem.at[0])
    share = pl.ds(pl.multiple_of(y * HSH, HSH), HSH)
    half_of = [pl.ds(pl.multiple_of((z % 2) * HALF, HALF), HALF), pl.ds(pl.multiple_of((1 - z % 2) * HALF, HALF), HALF)]
    own_h = pltpu.make_async_copy(h_ref.at[half_of[0], share], hc.at[x, half_of[0], share], lsem.at[1])
    own_t = pltpu.make_async_copy(t_ref.at[:, cols_of(x)], tc.at[x], lsem.at[2])
    all_t = pltpu.make_async_copy(t_ref, town, lsem.at[3])
    all_w = pltpu.make_async_copy(w_ref, wown, lsem.at[4])
    for cp in (own_h, all_t, all_w, own_w, own_t):
        cp.start()
    pl.semaphore_wait(barrier, len(partners))

    h_x = [
        remote(
            h_ref.at[half_of[0], share], hc.at[x, half_of[0], share], hxs.at[o - 1], hxr.at[o - 1], at_x(o)
        )
        for o in range(1, NX)
    ]
    w_x = [
        remote(
            w_ref.at[:, cols_of(lax.rem(x + o, NX))], wc.at[wrows(x, c)], wxs.at[o - 1], wxr.at[o - 1], at_x(o)
        )
        for o in range(1, NX)
    ]
    t_x = [
        remote(t_ref.at[:, cols_of(lax.rem(x + o, NX))], tc.at[x], ts.at[o - 1], tr.at[o - 1], at_x(o))
        for o in range(1, NX)
    ]

    def w_core(o):
        rows = wrows(lax.rem(x + NX - o, NX), c)
        src = w_ref.at[:, cols_of(x)] if o == 0 else wc.at[rows]
        return remote(src, wc.at[rows], wcs.at[o], wcr.at[o], other)

    w_c = [w_core(o) for o in range(NX)]
    for cp in h_x + w_x:
        cp.start()
    w_c[0].start()

    own_h.wait()
    for cp in h_x:
        cp.wait_recv()
    shares = [hc.at[:, rows, share] for rows in half_of]
    h_z = remote(shares[0], shares[0], hzs.at[0], hzr.at[0], beside)
    h_y = [
        [remote(part, part, hys.at[i, o - 1], hyr.at[i, o - 1], at_y(o)) for o in range(1, NY)]
        for i, part in enumerate(shares)
    ]
    h_z.start()
    for cp in h_y[0]:
        cp.start()

    for b in range(NX):
        sy[y, b] = jnp.where(lax.broadcasted_iota(jnp.int32, (8, BLK), 0) % 2 == 0, LOW, 0.0)
    all_t.wait()
    part = fold([town[:, 128 * g : 128 * g + 128] for g in range(COLS // 128)], jnp.maximum)
    top = jnp.max(part, axis=1, keepdims=True)
    total = fold([jnp.exp(town[:, 128 * g : 128 * g + 128] - top) for g in range(COLS // 128)], jnp.add)
    sy[y, x, 2:3, :] = row_max(part)
    sy[y, x, 3:4, :] = row_sum(total)

    all_w.wait()

    def turn(i, carry):
        cols = pl.ds(pl.multiple_of(i * 512, 512), 512)
        wt[cols, :] = wown[:, cols].T
        return carry

    lax.fori_loop(0, COLS // 512, turn, 0)

    h_z.wait_recv()
    for cp in h_y[1]:
        cp.start()
    for o in (1, 3, 2):
        w_x[o - 1].wait_recv()
        w_c[o].start()
    for cp in w_x:
        cp.wait_send()
    for cp in t_x:
        cp.start()
    for cp in h_y[0] + h_y[1]:
        cp.wait_recv()

    mine = pl.ds(pl.multiple_of(x * CHIP, CHIP), CHIP)
    h_c = remote(hc.at[:, :, mine], hx.at[c], hcs.at[0], hcr.at[0], other)
    h_c.start()
    keep = pltpu.make_async_copy(hc.at[:, :, mine], hx.at[c], lsem.at[5])
    keep.start()
    own_w.wait()
    for cp in w_c:
        cp.wait_recv()

    def score(i, carry):
        cols = pl.ds(pl.multiple_of(i * 256, 256), 256)
        tile = jnp.dot(hc[...].reshape(NX * BLK, D), wc[:, cols], preferred_element_type=F32)
        student[:, :, cols] = tile.reshape(NX, BLK, 256)
        return carry

    lax.fori_loop(0, PART // 256, score, 0)

    def local_stats(b, carry):
        parts = groups(student[b])
        part = fold(parts, jnp.maximum)
        top = jnp.max(part, axis=1, keepdims=True)
        total = fold([jnp.exp(p - top) for p in parts], jnp.add)
        sy[y, b, 0:1, :] = row_max(part)
        sy[y, b, 1:2, :] = row_sum(total)
        return carry

    lax.fori_loop(0, NX, local_stats, 0)

    def reduce_stats(slots, count, target):
        for b in range(NX):
            m_s = fold([slots[i, b, 0:1, :] for i in range(count)], jnp.maximum)
            m_t = fold([slots[i, b, 2:3, :] for i in range(count)], jnp.maximum)
            l_s = fold([slots[i, b, 1:2, :] * jnp.exp(slots[i, b, 0:1, :] - m_s) for i in range(count)], jnp.add)
            l_t = fold([slots[i, b, 3:4, :] * jnp.exp(slots[i, b, 2:3, :] - m_t) for i in range(count)], jnp.add)
            target(b, m_s, l_s, m_t, l_t)

    def into(slots, me):
        def put(b, *values):
            for r, value in enumerate(values):
                slots[me, b, r : r + 1, :] = value

        return put

    s_x = [remote(sx.at[x], sx.at[x], sxs.at[o - 1], sxr.at[o - 1], at_x(o)) for o in range(1, NX)]
    s_y = [remote(sy.at[y], sy.at[y], sys_.at[o - 1], syr.at[o - 1], at_y(o)) for o in range(1, NY)]
    s_z = [remote(sz.at[z], sz.at[z], szs.at[o - 1], szr.at[o - 1], at_z(o)) for o in range(1, NZ)]
    for cp in s_y:
        cp.start()
    for cp in s_y:
        cp.wait_recv()
    reduce_stats(sy, NY, into(sz, z))
    for cp in s_z:
        cp.start()
    for cp in s_z:
        cp.wait_recv()
    reduce_stats(sz, NZ, into(sx, x))
    for cp in s_x:
        cp.start()
    for cp in s_x:
        cp.wait_recv()
    def columns(b, m_s, l_s, m_t, l_t):
        for r, value in enumerate((m_s, loss_scale / l_s, m_t, loss_scale / l_t)):
            col[r, b] = jnp.broadcast_to(value, (BLK, BLK)).T
        last[b, 0:1, :] = m_s + jnp.log(l_s) - m_t - jnp.log(l_t)
        last[b, 1:2, :] = l_t

    reduce_stats(sx, NX, columns)

    own_t.wait()
    for cp in t_x:
        cp.wait_recv()

    def rows_at(s, plane):
        turn = STEPS[s][0]
        k = lax.rem(y + turn, NY) if plane == 0 else lax.rem(y + NY - turn, NY)
        return pl.ds(pl.multiple_of(k * SUB + STEPS[s][1], 16), STEPS[s][2])

    def rows_mine(s):
        turn = STEPS[s][0]
        k = lax.rem(y + turn + c * (2 * NY - 2 * turn), NY)
        return pl.ds(pl.multiple_of(k * SUB + STEPS[s][1], 16), STEPS[s][2])

    def piece(s, owner, part, parts):
        size = NX * STEPS[s][2]
        first = FIRST[s] + c * size + part * (size // parts)
        return gbuf.at[pl.ds(pl.multiple_of(first, 32), size // parts), cols_of(owner)]

    left, right, far = lax.rem(x + 3, NX), lax.rem(x + 1, NX), lax.rem(x + 2, NX)
    owners = [x, left, far, right]
    g_a, g_f, g_c = [], [], []
    for s in range(len(STEPS)):
        own, low, high = piece(s, x, 0, 1), piece(s, left, 0, 2), piece(s, right, 1, 2)
        g_a.append([remote(own, own, gas.at[s, i], gar.at[s, i], at_x(o)) for i, o in enumerate((1, 3))])
        g_f.append(
            [
                remote(low, low, gfs.at[s, 0], gfr.at[s, 0], at_x(1)),
                remote(high, high, gfs.at[s, 1], gfr.at[s, 1], at_x(3)),
            ]
        )
        blocks = [piece(s, q, 0, 1) for q in owners]
        g_c.append([remote(q, q, gcs.at[s, o], gcr.at[s, o], other) for o, q in enumerate(blocks)])

    def make(s):
        rows, count = rows_mine(s), STEPS[s][2]

        def grad(b, carry):
            m_s, a_s, m_t, a_t = [col[r, b, rows, :] for r in range(4)]
            out = pl.ds(pl.multiple_of(FIRST[s] + c * (NX * count) + b * count, 16), count)
            total = jnp.zeros((count, 128), F32)
            tiles = []
            for g in range(PART // 128):
                st = student[b, rows, 128 * g : 128 * g + 128]
                te = tc[b, rows, 128 * g : 128 * g + 128]
                e_t = jnp.exp(te - m_t)
                total += e_t * (te - st)
                tiles.append((jnp.exp(st - m_s) * a_s - e_t * a_t).astype(BF16))
            gbuf[out, cols_of(x)] = jnp.concatenate(tiles, axis=1)
            cross[b, rows, :] = total
            return carry

        lax.fori_loop(0, NX, grad, 0)

    def offer(s):
        for cp in g_a[s]:
            cp.start()
        g_c[s][0].start()

    def pass_on(s):
        for i, o in enumerate((1, 3)):
            g_a[s][i].wait_recv()
            g_f[s][i].start()
            g_c[s][o].start()

    make(0)
    offer(0)
    make(1)
    offer(1)
    for s in range(2, len(STEPS)):
        make(s)

    keep.wait()
    h_c.wait_recv()
    for s in range(len(STEPS)):
        count = STEPS[s][2]
        block = jnp.concatenate([hx[j, b, rows_at(s, j), :] for j in range(2) for b in range(NX)], axis=0)
        block = pltpu.roll(block.astype(F32), lax.rem(c * WID, CHIP), 1)[:, :512]
        ht[:, FIRST[s] : FIRST[s] + 2 * NX * count] = block.T[:WID].astype(BF16)

    for b in range(NX):
        cx[x, b] = jnp.broadcast_to(row_sum(cross[b]), (8, BLK))
    c_x = [
        remote(
            cx.at[x, lax.rem(x + o, NX)], cx.at[x, lax.rem(x + o, NX)], cxs.at[o - 1], cxr.at[o - 1], at_x(o)
        )
        for o in range(1, NX)
    ]
    c_y = [remote(cy.at[y], cy.at[y], cys.at[o - 1], cyr.at[o - 1], at_y(o)) for o in range(1, NY)]
    c_z = [remote(cz.at[z], cz.at[z], czs.at[o - 1], czr.at[o - 1], at_z(o)) for o in range(1, NZ)]

    h_to_y = [
        [
            remote(
                hgp.at[s, pl.ds(j * BLK, BLK)], hgy.at[s, pl.ds(j * BLK, BLK)],
                hgys.at[s, j], hgyr.at[s, j], at_y(s + 1 if j == 0 else 3 - s),
            )
            for j in range(2)
        ]
        for s in range(NY - 1)
    ]

    def z_rows(i, o):
        zz = lax.rem(z + o, NZ)
        return pl.ds(pl.multiple_of(i * BLK + (zz % 2) * 64 + (zz // 2) * 16, 16), 16)

    h_to_z = [
        [
            remote(
                hgp.at[3, z_rows(i, o)], hgz.at[o - 1, pl.ds(16 * i, 16)], hgzs.at[i, o - 1], hgzr.at[i, o - 1], at_z(o)
            )
            for o in range(1, NZ)
        ]
        for i in range(2)
    ]

    def complete(s):
        for cp in g_f[s]:
            cp.wait_recv()
        g_c[s][2].start()
        for cp in g_c[s]:
            cp.wait_recv()
        size = 2 * NX * STEPS[s][2]
        product = jnp.dot(gbuf[FIRST[s] : FIRST[s] + size], wt[...], preferred_element_type=F32)
        if s < 3:
            hgp[s] = product
            for cp in h_to_y[s]:
                cp.start()
            return
        i = s - 3
        if i == 0:
            for cp in sum(h_to_y, []):
                cp.wait_recv()
        for j in range(2):
            for b in range(NX):
                rows = slice(j * BLK + b * SUB + 16 * i, j * BLK + b * SUB + 16 * i + 16)
                at = slice(j * 64 + b * 16, j * 64 + b * 16 + 16)
                out = slice(i * BLK + at.start, i * BLK + at.stop)
                hgp[3, out] = product[at] + hgy[0, rows] + hgy[1, rows] + hgy[2, rows]
        for cp in h_to_z[i]:
            cp.start()

    def head_product(s):
        depth = slice(BIG * s, BIG * s + BIG)

        def head(i, carry):
            cols = pl.ds(pl.multiple_of(i * 512, 512), 512)
            tile = jnp.dot(ht[:, depth], gbuf[depth, cols], preferred_element_type=F32)
            if s == 0:
                acc[:, cols] = tile
            elif s < 3:
                acc[:, cols] += tile
            else:
                dw_ref[:, cols] = (acc[:, cols] + tile).astype(BF16)
            return carry

        lax.fori_loop(0, COLS // 512, head, 0)

    pass_on(0)
    offer(2)
    pass_on(1)
    offer(3)
    for cp in c_x:
        cp.start()
    complete(0)
    head_product(0)
    pass_on(2)
    offer(4)
    for cp in c_x:
        cp.wait_recv()
    cy[y] = cx[0, x] + cx[1, x] + cx[2, x] + cx[3, x]
    for cp in c_y:
        cp.start()
    complete(1)
    head_product(1)
    pass_on(3)
    for cp in c_y:
        cp.wait_recv()
    cz[z] = cy[0] + cy[1] + cy[2] + cy[3]
    for cp in c_z:
        cp.start()
    complete(2)
    head_product(2)
    pass_on(4)
    complete(3)
    complete(4)
    head_product(3)

    for cp in c_z:
        cp.wait_recv()
    crossed = fold([cz[i, 0:1, :] for i in range(NZ)], jnp.add)
    div_ref[...] = crossed / last[x, 1:2, :] + last[x, 0:1, :]

    for i in range(2):
        for cp in h_to_z[i]:
            cp.wait_recv()
        total = hgp[3, z_rows(i, 0), :]
        for o in range(NZ - 1):
            total = total + hgz[o, 16 * i : 16 * i + 16]
        hg_ref[16 * i : 16 * i + 16, :] = total.astype(BF16)

    sent = h_x + [h_z, h_c] + w_c + t_x + s_x + s_y + s_z + c_x + c_y + c_z
    for cp in sent + sum(h_y + g_a + g_f + g_c + h_to_y + h_to_z, []):
        cp.wait_send()


def put(div_in, hg_in, dw_in, div_ref, hg_ref, dw_ref, sems):
    rows = WID // 7
    parts = [pl.ds(rows * i, rows) for i in range(7)]
    copies = [pltpu.make_async_copy(dw_in.at[p], dw_ref.at[p], sems.at[i]) for i, p in enumerate(parts)]
    for cp in copies:
        cp.start()
    div_ref[...] = div_in[0]
    hg_ref[...] = hg_in[...]
    for cp in copies:
        cp.wait()


def local(hidden, head_weight, teacher_logits):
    dma = pltpu.SemaphoreType.DMA
    vmem = pltpu.VMEM
    scratch = [
        vmem((NX, BLK, D), BF16),
        vmem((D, PART), BF16),
        vmem((NX, BLK, PART), F32),
        vmem((NX, BLK, PART), F32),
        vmem((BLK, COLS), F32),
        vmem((WID, COLS), BF16),
        vmem((COLS, WID), BF16),
        vmem((2, NX, BLK, CHIP), BF16),
        vmem((WID, ROWS), BF16),
        vmem((ROWS, COLS), BF16),
        vmem((WID, COLS), F32),
        vmem((NY, 2 * BLK, WID), F32),
        vmem((NY - 1, 2 * BLK, WID), F32),
        vmem((NZ - 1, SUB, WID), F32),
        vmem((NX, NX, 8, BLK), F32),
        vmem((NY, NX, 8, BLK), F32),
        vmem((NZ, NX, 8, BLK), F32),
        vmem((NX, 8, BLK), F32),
        vmem((4, NX, BLK, BLK), F32),
        vmem((NX, BLK, BLK), F32),
        vmem((NX, NX, 8, BLK), F32),
        vmem((NY, 8, BLK), F32),
        vmem((NZ, 8, BLK), F32),
    ]
    counts = [(3,), (1,), (2, 3), (3,), (4,), (3,), (1,), (3,), (3,), (7,)]
    counts += [(5, 2), (5, 2), (5, 4), (3, 2), (2, 7), (3,), (3,), (7,)]
    sems = [dma((6,))]
    for n in counts:
        sems += [dma(n), dma(n)]
    div, hg, dw = pl.pallas_call(
        kernel,
        name="distill",
        out_shape=(vmem((1, BLK), F32), vmem((SUB, WID), BF16), vmem((WID, COLS), BF16)),
        in_specs=[pl.BlockSpec(memory_space=pl.ANY)] * 3,
        out_specs=[pl.BlockSpec(memory_space=vmem)] * 3,
        scratch_shapes=scratch + sems,
        compiler_params=pltpu.CompilerParams(
            collective_id=0, has_side_effects=True, vmem_limit_bytes=54 * 1024 * 1024
        ),
    )(hidden, head_weight, teacher_logits)
    div, hg, dw = pl.pallas_call(
        put,
        name="put",
        out_shape=(
            jax.ShapeDtypeStruct((BLK,), F32),
            jax.ShapeDtypeStruct((SUB, WID), BF16),
            jax.ShapeDtypeStruct((WID, COLS), BF16),
        ),
        in_specs=[pl.BlockSpec(memory_space=vmem)] * 3,
        out_specs=[pl.BlockSpec(memory_space=vmem)] * 2 + [pl.BlockSpec(memory_space=pl.ANY)],
        scratch_shapes=[dma((7,))],
    )(div, hg, dw)
    return div, hg, dw


def solution(mesh):
    return jax.shard_map(
        local,
        mesh=mesh,
        in_specs=(P("dp", None), P("dp", "vocab"), P("dp", "vocab")),
        out_specs=(P("dp"), P("vocab", "dp"), P("dp", "vocab")),
        check_vma=False,
    )
```

time: 183 us -> 156 us (0.85)
  Pallas kernels: 173 us -> 151 us
  local copies, waits for them, and re-layouts: 6.79 us -> 2.85 us
    pallas_call x1 -> x2, Pallas kernels: 173 us -> 151 us  [the longest x1 146 us: local(): pl.pallas_call(kernel, name='distill', out_shape=(vmem((1, BLK), F32), vm...]
    unnamed x3 -> x6, local copies, waits for them, and re-layouts: 6.79 us -> 2.85 us
where the time goes in v2:
time: 156 us; the launch traced here: 154 us
  Pallas kernels  151 us (97%)
  local copies, waits for them, and re-layouts  2.85 us (2%)
    pallas_call x1, Pallas kernels, local(): pl.pallas_call(kernel, name='distill', out_shape=(vmem((1, BLK), F32), vm...  146 us
    pallas_call x1, Pallas kernels, local(): pl.pallas_call(put, name='put', out_shape=(jax.ShapeDtypeStruct((BLK,), F...  4.57 us

profile of v2, /device:TPU:24, one launch (start us, length us, event | category | flops | bytes accessed | tf_op | source)
XLA Modules:
  0.0 154.0 jit_solution(2460282360037760880)
XLA Ops:
  0.6 145.9 %distill.1 = (f32[1,128]{1,0:T(1,128)S(1)}, bf16[32,448]{1,0:T(8,128)(2,1)S(1)}, bf16[448,4096]{1,0:T(8,128)(2,1)S(1)}) custom-call(bf16[128,3584]{1,0:T(8,128)(2,1)} %h_ref.1, bf16[448,4096]{1,0:T(8,128)(2,1)} %w_ref.1, f32[128,4096]{1,0:T(8,128)} %t_ref.1), custom_call_target="tpu_custom_call" | custom-call | tf_op jit(solution)/shard_map/distill/pallas_call | solution.py:491
  146.6 0.0 copy-start
  146.6 1.8 %copy-done = bf16[448,4096]{1,0:T(8,128)(2,1)} copy-done((bf16[448,4096]{1,0:T(8,128)(2,1)}, bf16[448,4096]{1,0:T(8,128)(2,1)S(1)}, u32[]{:S(2)}) %copy-start) | copy-done | bytes 3670040
  148.4 0.0 copy-start.1
  148.4 0.6 copy-done.1
  149.0 0.0 copy-start.2
  149.0 0.5 copy-done.2
  149.4 4.6 %put.1 = (f32[128]{0:T(128)}, bf16[32,448]{1,0:T(8,128)(2,1)}, bf16[448,4096]{1,0:T(8,128)(2,1)}) custom-call(f32[1,128]{1,0:T(1,128)} %copy-done.2, bf16[32,448]{1,0:T(8,128)(2,1)} %copy-done.1, bf16[448,4096]{1,0:T(8,128)(2,1)} %copy-done), custom_call_target="tpu_custom_call" | custom-call | tf_op jit(solution)/shard_map/put/pallas_call | solution.py:502
Async XLA Ops:
  146.6 1.8 %copy-start = (bf16[448,4096]{1,0:T(8,128)(2,1)}, bf16[448,4096]{1,0:T(8,128)(2,1)S(1)}, u32[]{:S(2)}) copy-start(bf16[448,4096]{1,0:T(8,128)(2,1)S(1)} %get-tuple-element.8.dw_in) | copy-start | bytes 11010052
  148.4 0.6 copy-start.1
  149.0 0.5 copy-start.2

commit v3 on v2

--- a/solution.py
+++ b/solution.py
@@ -22,9 +22,11 @@
 HALF = BLK // 2
 
 
-STEPS = ((1, 0, 32), (2, 0, 32), (3, 0, 32), (0, 0, 16), (0, 16, 16))
-BIG = 2 * NX * SUB
-FIRST = (0, BIG, 2 * BIG, 3 * BIG, 3 * BIG + BIG // 2)
+STEPS = tuple((turn, first, 16) for first in (0, 16) for turn in (1, 2, 3, 0))
+FIRST = tuple(128 * s for s in range(8))
+EARLY = 112
+WIDE = 512
+AHEAD = 3
 
 
 def groups(value):
@@ -93,7 +95,7 @@
     own_h = pltpu.make_async_copy(h_ref.at[half_of[0], share], hc.at[x, half_of[0], share], lsem.at[1])
     own_t = pltpu.make_async_copy(t_ref.at[:, cols_of(x)], tc.at[x], lsem.at[2])
     all_t = pltpu.make_async_copy(t_ref, town, lsem.at[3])
-    all_w = pltpu.make_async_copy(w_ref, wown, lsem.at[4])
+    all_w = pltpu.make_async_copy(w_ref, wown.at[pl.ds(0, WID)], lsem.at[4])
     for cp in (own_h, all_t, all_w, own_w, own_t):
         cp.start()
     pl.semaphore_wait(barrier, len(partners))
@@ -111,8 +113,13 @@
         for o in range(1, NX)
     ]
     t_x = [
-        remote(t_ref.at[:, cols_of(lax.rem(x + o, NX))], tc.at[x], ts.at[o - 1], tr.at[o - 1], at_x(o))
-        for o in range(1, NX)
+        [
+            remote(
+                t_ref.at[rows, cols_of(lax.rem(x + o, NX))], tc.at[x, rows], ts.at[i, o - 1], tr.at[i, o - 1], at_x(o)
+            )
+            for o in range(1, NX)
+        ]
+        for i, rows in enumerate((pl.ds(0, EARLY), pl.ds(EARLY, BLK - EARLY)))
     ]
 
     def w_core(o):
@@ -148,6 +155,7 @@
     sy[y, x, 3:4, :] = row_sum(total)
 
     all_w.wait()
+    wown[WID:] = jnp.zeros((WIDE - WID, COLS), BF16)
 
     def turn(i, carry):
         cols = pl.ds(pl.multiple_of(i * 512, 512), 512)
@@ -164,7 +172,7 @@
         w_c[o].start()
     for cp in w_x:
         cp.wait_send()
-    for cp in t_x:
+    for cp in t_x[0]:
         cp.start()
     for cp in h_y[0] + h_y[1]:
         cp.wait_recv()
@@ -225,7 +233,7 @@
     for cp in s_z:
         cp.wait_recv()
     reduce_stats(sz, NZ, into(sx, x))
-    for cp in s_x:
+    for cp in s_x + t_x[1]:
         cp.start()
     for cp in s_x:
         cp.wait_recv()
@@ -238,7 +246,7 @@
     reduce_stats(sx, NX, columns)
 
     own_t.wait()
-    for cp in t_x:
+    for cp in t_x[0] + t_x[1]:
         cp.wait_recv()
 
     def rows_at(s, plane):
@@ -302,12 +310,10 @@
             g_f[s][i].start()
             g_c[s][o].start()
 
-    make(0)
-    offer(0)
-    make(1)
-    offer(1)
-    for s in range(2, len(STEPS)):
+    for s in range(len(STEPS)):
         make(s)
+        if s < AHEAD:
+            offer(s)
 
     keep.wait()
     h_c.wait_recv()
@@ -328,102 +334,86 @@
     c_y = [remote(cy.at[y], cy.at[y], cys.at[o - 1], cyr.at[o - 1], at_y(o)) for o in range(1, NY)]
     c_z = [remote(cz.at[z], cz.at[z], czs.at[o - 1], czr.at[o - 1], at_z(o)) for o in range(1, NZ)]
 
-    h_to_y = [
-        [
-            remote(
-                hgp.at[s, pl.ds(j * BLK, BLK)], hgy.at[s, pl.ds(j * BLK, BLK)],
-                hgys.at[s, j], hgyr.at[s, j], at_y(s + 1 if j == 0 else 3 - s),
-            )
-            for j in range(2)
-        ]
-        for s in range(NY - 1)
-    ]
-
-    def z_rows(i, o):
+    def to_y(s, j):
+        rows = pl.ds(s * BLK + j * 64, 64)
+        up = STEPS[s][0] if j == 0 else NY - STEPS[s][0]
+        return remote(hgp.at[rows], hgy.at[rows], hgys.at[s, j], hgyr.at[s, j], at_y(up))
+
+    def to_z(i, o):
         zz = lax.rem(z + o, NZ)
-        return pl.ds(pl.multiple_of(i * BLK + (zz % 2) * 64 + (zz // 2) * 16, 16), 16)
-
-    h_to_z = [
-        [
-            remote(
-                hgp.at[3, z_rows(i, o)], hgz.at[o - 1, pl.ds(16 * i, 16)], hgzs.at[i, o - 1], hgzr.at[i, o - 1], at_z(o)
-            )
-            for o in range(1, NZ)
-        ]
-        for i in range(2)
-    ]
-
-    def complete(s):
+        rows = pl.ds(pl.multiple_of((4 * i + 3) * BLK + (zz % 2) * 64 + (zz // 2) * 16, 16), 16)
+        return remote(hgp.at[rows], hgz.at[o - 1, pl.ds(16 * i, 16)], hgzs.at[i, o - 1], hgzr.at[i, o - 1], at_z(o))
+
+    h_to_y = [[to_y(s, j) for j in range(2)] if STEPS[s][0] else [] for s in range(len(STEPS))]
+    h_to_z = [[to_z(i, o) for o in range(1, NZ)] for i in range(2)]
+
+    def far_in(s):
         for cp in g_f[s]:
             cp.wait_recv()
         g_c[s][2].start()
+
+    def product(s):
         for cp in g_c[s]:
             cp.wait_recv()
-        size = 2 * NX * STEPS[s][2]
-        product = jnp.dot(gbuf[FIRST[s] : FIRST[s] + size], wt[...], preferred_element_type=F32)
-        if s < 3:
-            hgp[s] = product
-            for cp in h_to_y[s]:
-                cp.start()
-            return
-        i = s - 3
-        if i == 0:
-            for cp in sum(h_to_y, []):
-                cp.wait_recv()
-        for j in range(2):
-            for b in range(NX):
-                rows = slice(j * BLK + b * SUB + 16 * i, j * BLK + b * SUB + 16 * i + 16)
-                at = slice(j * 64 + b * 16, j * 64 + b * 16 + 16)
-                out = slice(i * BLK + at.start, i * BLK + at.stop)
-                hgp[3, out] = product[at] + hgy[0, rows] + hgy[1, rows] + hgy[2, rows]
+        rows = slice(FIRST[s], FIRST[s] + BLK)
+        hgp[rows] = jnp.dot(gbuf[rows], wt[...], preferred_element_type=F32)
+        for cp in h_to_y[s]:
+            cp.start()
+
+    def gather_z(i):
+        for cp in sum(h_to_y[4 * i : 4 * i + 3], []):
+            cp.wait_recv()
+        at = [slice((4 * i + t) * BLK, (4 * i + t + 1) * BLK) for t in range(4)]
+        hgp[at[3]] += hgy[at[0]] + hgy[at[1]] + hgy[at[2]]
         for cp in h_to_z[i]:
             cp.start()
 
-    def head_product(s):
-        depth = slice(BIG * s, BIG * s + BIG)
-
-        def head(i, carry):
-            cols = pl.ds(pl.multiple_of(i * 512, 512), 512)
+    def head_product(i, first, last):
+        depth = slice(512 * i, 512 * i + 512)
+
+        def head(n, carry):
+            cols = pl.ds(pl.multiple_of(n * 512, 512), 512)
             tile = jnp.dot(ht[:, depth], gbuf[depth, cols], preferred_element_type=F32)
-            if s == 0:
+            if i == 0:
                 acc[:, cols] = tile
-            elif s < 3:
-                acc[:, cols] += tile
             else:
                 dw_ref[:, cols] = (acc[:, cols] + tile).astype(BF16)
             return carry
 
-        lax.fori_loop(0, COLS // 512, head, 0)
-
-    pass_on(0)
-    offer(2)
-    pass_on(1)
-    offer(3)
-    for cp in c_x:
-        cp.start()
-    complete(0)
-    head_product(0)
-    pass_on(2)
-    offer(4)
-    for cp in c_x:
-        cp.wait_recv()
-    cy[y] = cx[0, x] + cx[1, x] + cx[2, x] + cx[3, x]
-    for cp in c_y:
-        cp.start()
-    complete(1)
-    head_product(1)
-    pass_on(3)
-    for cp in c_y:
-        cp.wait_recv()
-    cz[z] = cy[0] + cy[1] + cy[2] + cy[3]
-    for cp in c_z:
-        cp.start()
-    complete(2)
-    head_product(2)
-    pass_on(4)
-    complete(3)
-    complete(4)
-    head_product(3)
+        lax.fori_loop(first, last, head, 0)
+
+    for s in range(len(STEPS)):
+        pass_on(s)
+        if s + AHEAD < len(STEPS):
+            offer(s + AHEAD)
+        if s == 1:
+            for cp in c_x:
+                cp.start()
+        if s == 3:
+            for cp in c_x:
+                cp.wait_recv()
+            cy[y] = cx[0, x] + cx[1, x] + cx[2, x] + cx[3, x]
+            for cp in c_y:
+                cp.start()
+        if s == 5:
+            for cp in c_y:
+                cp.wait_recv()
+            cz[z] = cy[0] + cy[1] + cy[2] + cy[3]
+            for cp in c_z:
+                cp.start()
+        if s >= 3:
+            product(s - 3)
+        if s >= 2:
+            far_in(s - 2)
+    product(5)
+    far_in(6)
+    product(6)
+    gather_z(0)
+    far_in(7)
+    product(7)
+    gather_z(1)
+    head_product(0, 0, 8)
+    head_product(1, 0, 8)
 
     for cp in c_z:
         cp.wait_recv()
@@ -433,13 +423,14 @@
     for i in range(2):
         for cp in h_to_z[i]:
             cp.wait_recv()
-        total = hgp[3, z_rows(i, 0), :]
+        mine = pl.ds(pl.multiple_of((4 * i + 3) * BLK + (z % 2) * 64 + (z // 2) * 16, 16), 16)
+        total = hgp[mine, :]
         for o in range(NZ - 1):
             total = total + hgz[o, 16 * i : 16 * i + 16]
-        hg_ref[16 * i : 16 * i + 16, :] = total.astype(BF16)
-
-    sent = h_x + [h_z, h_c] + w_c + t_x + s_x + s_y + s_z + c_x + c_y + c_z
-    for cp in sent + sum(h_y + g_a + g_f + g_c + h_to_y + h_to_z, []):
+        hg_ref[16 * i : 16 * i + 16, :] = total[:, :WID].astype(BF16)
+
+    sent = h_x + [h_z, h_c] + w_c + s_x + s_y + s_z + c_x + c_y + c_z
+    for cp in sent + sum(h_y + t_x + g_a + g_f + g_c + h_to_y + h_to_z, []):
         cp.wait_send()
 
 
@@ -464,15 +455,15 @@
         vmem((NX, BLK, PART), F32),
         vmem((NX, BLK, PART), F32),
         vmem((BLK, COLS), F32),
-        vmem((WID, COLS), BF16),
-        vmem((COLS, WID), BF16),
+        vmem((WIDE, COLS), BF16),
+        vmem((COLS, WIDE), BF16),
         vmem((2, NX, BLK, CHIP), BF16),
         vmem((WID, ROWS), BF16),
         vmem((ROWS, COLS), BF16),
         vmem((WID, COLS), F32),
-        vmem((NY, 2 * BLK, WID), F32),
-        vmem((NY - 1, 2 * BLK, WID), F32),
-        vmem((NZ - 1, SUB, WID), F32),
+        vmem((ROWS, WIDE), F32),
+        vmem((ROWS, WIDE), F32),
+        vmem((NZ - 1, SUB, WIDE), F32),
         vmem((NX, NX, 8, BLK), F32),
         vmem((NY, NX, 8, BLK), F32),
         vmem((NZ, NX, 8, BLK), F32),
@@ -483,8 +474,8 @@
         vmem((NY, 8, BLK), F32),
         vmem((NZ, 8, BLK), F32),
     ]
-    counts = [(3,), (1,), (2, 3), (3,), (4,), (3,), (1,), (3,), (3,), (7,)]
-    counts += [(5, 2), (5, 2), (5, 4), (3, 2), (2, 7), (3,), (3,), (7,)]
+    counts = [(3,), (1,), (2, 3), (3,), (4,), (2, 3), (1,), (3,), (3,), (7,)]
+    counts += [(8, 2), (8, 2), (8, 4), (8, 2), (2, 7), (3,), (3,), (7,)]
     sems = [dma((6,))]
     for n in counts:
         sems += [dma(n), dma(n)]
@@ -510,6 +501,7 @@
         in_specs=[pl.BlockSpec(memory_space=vmem)] * 3,
         out_specs=[pl.BlockSpec(memory_space=vmem)] * 2 + [pl.BlockSpec(memory_space=pl.ANY)],
         scratch_shapes=[dma((7,))],
+        compiler_params=pltpu.CompilerParams(vmem_limit_bytes=2 * 1024 * 1024),
     )(div, hg, dw)
     return div, hg, dw
 

time: 156 us -> 142 us (0.910)
  Pallas kernels: 151 us -> 139 us
  local copies, waits for them, and re-layouts: 2.85 us -> 0 us
    pallas_call x1, Pallas kernels: 146 us -> 137 us  [local(): pl.pallas_call(kernel, name='distill', out_shape=(vmem((1, BLK), F32), vm...]
    unnamed x6 -> x0, local copies, waits for them, and re-layouts: 2.85 us -> none
    pallas_call x1, Pallas kernels: 4.57 us -> 2.51 us  [local(): pl.pallas_call(put, name='put', out_shape=(jax.ShapeDtypeStruct((BLK,), F...]
where the time goes in v3:
time: 142 us; the launch traced here: 140 us
  Pallas kernels  139 us (98%)
    pallas_call x1, Pallas kernels, local(): pl.pallas_call(kernel, name='distill', out_shape=(vmem((1, BLK), F32), vm...  137 us

profile of v3, /device:TPU:24, one launch (start us, length us, event | category | flops | bytes accessed | tf_op | source)
XLA Modules:
  0.0 139.9 jit_solution(3893290922229795891)
XLA Ops:
  0.6 136.7 %distill.1 = (f32[1,128]{1,0:T(1,128)S(1)}, bf16[32,448]{1,0:T(8,128)(2,1)S(1)}, bf16[448,4096]{1,0:T(8,128)(2,1)S(1)}) custom-call(bf16[128,3584]{1,0:T(8,128)(2,1)} %h_ref.1, bf16[448,4096]{1,0:T(8,128)(2,1)} %w_ref.1, f32[128,4096]{1,0:T(8,128)} %t_ref.1), custom_call_target="tpu_custom_call" | custom-call | tf_op jit(solution)/shard_map/distill/pallas_call | solution.py:482
  137.4 2.5 %put.1 = (f32[128]{0:T(128)}, bf16[32,448]{1,0:T(8,128)(2,1)}, bf16[448,4096]{1,0:T(8,128)(2,1)}) custom-call(f32[1,128]{1,0:T(1,128)S(1)} %get-tuple-element.6.div_in, bf16[32,448]{1,0:T(8,128)(2,1)S(1)} %get-tuple-element.7.hg_in, bf16[448,4096]{1,0:T(8,128)(2,1)S(1)} %get-tuple-element.8.dw_in), custom_call_target="tpu_custom_call" | custom-call | tf_op jit(solution)/shard_map/put/pallas_call | solution.py:493

commit v4 on v3

--- a/solution.py
+++ b/solution.py
@@ -22,11 +22,13 @@
 HALF = BLK // 2
 
 
-STEPS = tuple((turn, first, 16) for first in (0, 16) for turn in (1, 2, 3, 0))
+STEPS = tuple((turn, first, 16) for turn, first in zip((3, 2, 3, 1, 2, 0, 1, 0), (0, 0, 16, 0, 16, 0, 16, 16)))
+BEFORE = (None, 0, None, 1, 2, 3, 4, 6)
+LAST = (5, 7)
 FIRST = tuple(128 * s for s in range(8))
 EARLY = 112
 WIDE = 512
-AHEAD = 3
+OFFERS = {0: 3, 2: 4, 3: 5, 4: 6, 6: 7}
 
 
 def groups(value):
@@ -310,21 +312,24 @@
             g_f[s][i].start()
             g_c[s][o].start()
 
-    for s in range(len(STEPS)):
+    make(0)
+    offer(0)
+    for s in range(1, len(STEPS)):
         make(s)
-        if s < AHEAD:
-            offer(s)
+    for b in range(NX):
+        cx[x, b] = jnp.broadcast_to(row_sum(cross[b]), (8, BLK))
+    offer(1)
 
     keep.wait()
     h_c.wait_recv()
     for s in range(len(STEPS)):
+        if s == 4:
+            offer(2)
         count = STEPS[s][2]
         block = jnp.concatenate([hx[j, b, rows_at(s, j), :] for j in range(2) for b in range(NX)], axis=0)
         block = pltpu.roll(block.astype(F32), lax.rem(c * WID, CHIP), 1)[:, :512]
         ht[:, FIRST[s] : FIRST[s] + 2 * NX * count] = block.T[:WID].astype(BF16)
 
-    for b in range(NX):
-        cx[x, b] = jnp.broadcast_to(row_sum(cross[b]), (8, BLK))
     c_x = [
         remote(
             cx.at[x, lax.rem(x + o, NX)], cx.at[x, lax.rem(x + o, NX)], cxs.at[o - 1], cxr.at[o - 1], at_x(o)
@@ -336,12 +341,11 @@
 
     def to_y(s, j):
         rows = pl.ds(s * BLK + j * 64, 64)
-        up = STEPS[s][0] if j == 0 else NY - STEPS[s][0]
-        return remote(hgp.at[rows], hgy.at[rows], hgys.at[s, j], hgyr.at[s, j], at_y(up))
+        return remote(hgp.at[rows], hgy.at[rows], hgys.at[s, j], hgyr.at[s, j], at_y(NY - 1 if j else 1))
 
     def to_z(i, o):
         zz = lax.rem(z + o, NZ)
-        rows = pl.ds(pl.multiple_of((4 * i + 3) * BLK + (zz % 2) * 64 + (zz // 2) * 16, 16), 16)
+        rows = pl.ds(pl.multiple_of(LAST[i] * BLK + (zz % 2) * 64 + (zz // 2) * 16, 16), 16)
         return remote(hgp.at[rows], hgz.at[o - 1, pl.ds(16 * i, 16)], hgzs.at[i, o - 1], hgzr.at[i, o - 1], at_z(o))
 
     h_to_y = [[to_y(s, j) for j in range(2)] if STEPS[s][0] else [] for s in range(len(STEPS))]
@@ -357,15 +361,11 @@
             cp.wait_recv()
         rows = slice(FIRST[s], FIRST[s] + BLK)
         hgp[rows] = jnp.dot(gbuf[rows], wt[...], preferred_element_type=F32)
-        for cp in h_to_y[s]:
-            cp.start()
-
-    def gather_z(i):
-        for cp in sum(h_to_y[4 * i : 4 * i + 3], []):
-            cp.wait_recv()
-        at = [slice((4 * i + t) * BLK, (4 * i + t + 1) * BLK) for t in range(4)]
-        hgp[at[3]] += hgy[at[0]] + hgy[at[1]] + hgy[at[2]]
-        for cp in h_to_z[i]:
+        if BEFORE[s] is not None:
+            for cp in h_to_y[BEFORE[s]]:
+                cp.wait_recv()
+            hgp[rows] += hgy[FIRST[BEFORE[s]] : FIRST[BEFORE[s]] + BLK]
+        for cp in h_to_y[s] or h_to_z[LAST.index(s)]:
             cp.start()
 
     def head_product(i, first, last):
@@ -382,37 +382,51 @@
 
         lax.fori_loop(first, last, head, 0)
 
-    for s in range(len(STEPS)):
+    def near(s):
         pass_on(s)
-        if s + AHEAD < len(STEPS):
-            offer(s + AHEAD)
-        if s == 1:
-            for cp in c_x:
-                cp.start()
-        if s == 3:
-            for cp in c_x:
-                cp.wait_recv()
-            cy[y] = cx[0, x] + cx[1, x] + cx[2, x] + cx[3, x]
-            for cp in c_y:
-                cp.start()
-        if s == 5:
-            for cp in c_y:
-                cp.wait_recv()
-            cz[z] = cy[0] + cy[1] + cy[2] + cy[3]
-            for cp in c_z:
-                cp.start()
-        if s >= 3:
-            product(s - 3)
-        if s >= 2:
-            far_in(s - 2)
+        if s in OFFERS:
+            offer(OFFERS[s])
+
+    near(0)
+    near(1)
+    for cp in c_x:
+        cp.start()
+    near(2)
+    far_in(0)
+    product(0)
+    far_in(1)
+    near(3)
+    far_in(2)
+    product(1)
+    for cp in c_x:
+        cp.wait_recv()
+    cy[y] = cx[0, x] + cx[1, x] + cx[2, x] + cx[3, x]
+    for cp in c_y:
+        cp.start()
+    near(4)
+    product(2)
+    far_in(3)
+    product(3)
+    head_product(0, 0, 2)
+    far_in(4)
+    near(5)
+    near(6)
+    for cp in c_y:
+        cp.wait_recv()
+    cz[z] = cy[0] + cy[1] + cy[2] + cy[3]
+    for cp in c_z:
+        cp.start()
+    product(4)
+    far_in(5)
+    head_product(0, 2, 4)
     product(5)
     far_in(6)
+    near(7)
     product(6)
-    gather_z(0)
+    head_product(0, 4, 6)
     far_in(7)
     product(7)
-    gather_z(1)
-    head_product(0, 0, 8)
+    head_product(0, 6, 8)
     head_product(1, 0, 8)
 
     for cp in c_z:
@@ -423,7 +437,7 @@
     for i in range(2):
         for cp in h_to_z[i]:
             cp.wait_recv()
-        mine = pl.ds(pl.multiple_of((4 * i + 3) * BLK + (z % 2) * 64 + (z // 2) * 16, 16), 16)
+        mine = pl.ds(pl.multiple_of(LAST[i] * BLK + (z % 2) * 64 + (z // 2) * 16, 16), 16)
         total = hgp[mine, :]
         for o in range(NZ - 1):
             total = total + hgz[o, 16 * i : 16 * i + 16]

time: 142 us -> 136 us (0.958); the launches traced: 140 us -> 136 us
  Pallas kernels: 139 us -> 136 us
    pallas_call x1, Pallas kernels: 137 us -> 133 us  [local(): pl.pallas_call(kernel, name='distill', out_shape=(vmem((1, BLK), F32), vm...]
where the time goes in v4:
time: 136 us
  Pallas kernels  136 us (100%)
    pallas_call x1, Pallas kernels, local(): pl.pallas_call(kernel, name='distill', out_shape=(vmem((1, BLK), F32), vm...  133 us

profile of v4, /device:TPU:24, one launch (start us, length us, event | category | flops | bytes accessed | tf_op | source)
XLA Modules:
  0.0 136.2 jit_solution(13310642368763339673)
XLA Ops:
  0.6 133.0 %distill.1 = (f32[1,128]{1,0:T(1,128)S(1)}, bf16[32,448]{1,0:T(8,128)(2,1)S(1)}, bf16[448,4096]{1,0:T(8,128)(2,1)S(1)}) custom-call(bf16[128,3584]{1,0:T(8,128)(2,1)} %h_ref.1, bf16[448,4096]{1,0:T(8,128)(2,1)} %w_ref.1, f32[128,4096]{1,0:T(8,128)} %t_ref.1), custom_call_target="tpu_custom_call" | custom-call | tf_op jit(solution)/shard_map/distill/pallas_call | solution.py:496
  133.7 2.5 %put.1 = (f32[128]{0:T(128)}, bf16[32,448]{1,0:T(8,128)(2,1)}, bf16[448,4096]{1,0:T(8,128)(2,1)}) custom-call(f32[1,128]{1,0:T(1,128)S(1)} %get-tuple-element.6.div_in, bf16[32,448]{1,0:T(8,128)(2,1)S(1)} %get-tuple-element.7.hg_in, bf16[448,4096]{1,0:T(8,128)(2,1)S(1)} %get-tuple-element.8.dw_in), custom_call_target="tpu_custom_call" | custom-call | tf_op jit(solution)/shard_map/put/pallas_call | solution.py:507

commit v5 on v4

--- a/solution.py
+++ b/solution.py
@@ -19,7 +19,7 @@
 COLS = 4096
 PART = COLS // NX
 HSH = D // NY
-HALF = BLK // 2
+THIN = BLK // NZ
 
 
 STEPS = tuple((turn, first, 16) for turn, first in zip((3, 2, 3, 1, 2, 0, 1, 0), (0, 0, 16, 0, 16, 0, 16, 16)))
@@ -72,7 +72,6 @@
         return (dp, lax.rem(z + o, NZ) * NY + y)
 
     other = (x * 2 + 1 - c, v)
-    beside = (dp, (z + 1 - 2 * (z % 2)) * NY + y)
 
     def remote(src, dst, ss, rs, device):
         return pltpu.make_async_remote_copy(
@@ -93,8 +92,8 @@
 
     own_w = pltpu.make_async_copy(w_ref.at[:, cols_of(x)], wc.at[wrows(x, c)], lsem.at[0])
     share = pl.ds(pl.multiple_of(y * HSH, HSH), HSH)
-    half_of = [pl.ds(pl.multiple_of((z % 2) * HALF, HALF), HALF), pl.ds(pl.multiple_of((1 - z % 2) * HALF, HALF), HALF)]
-    own_h = pltpu.make_async_copy(h_ref.at[half_of[0], share], hc.at[x, half_of[0], share], lsem.at[1])
+    thin = [pl.ds(pl.multiple_of(lax.rem(z + NZ - o, NZ) * THIN, THIN), THIN) for o in range(NZ)]
+    own_h = pltpu.make_async_copy(h_ref.at[thin[0], share], hc.at[x, thin[0], share], lsem.at[1])
     own_t = pltpu.make_async_copy(t_ref.at[:, cols_of(x)], tc.at[x], lsem.at[2])
     all_t = pltpu.make_async_copy(t_ref, town, lsem.at[3])
     all_w = pltpu.make_async_copy(w_ref, wown.at[pl.ds(0, WID)], lsem.at[4])
@@ -104,7 +103,7 @@
 
     h_x = [
         remote(
-            h_ref.at[half_of[0], share], hc.at[x, half_of[0], share], hxs.at[o - 1], hxr.at[o - 1], at_x(o)
+            h_ref.at[thin[0], share], hc.at[x, thin[0], share], hxs.at[o - 1], hxr.at[o - 1], at_x(o)
         )
         for o in range(1, NX)
     ]
@@ -137,14 +136,14 @@
     own_h.wait()
     for cp in h_x:
         cp.wait_recv()
-    shares = [hc.at[:, rows, share] for rows in half_of]
-    h_z = remote(shares[0], shares[0], hzs.at[0], hzr.at[0], beside)
+    shares = [hc.at[:, rows, share] for rows in thin]
+    h_z = [remote(shares[0], shares[0], hzs.at[o - 1], hzr.at[o - 1], at_z(o)) for o in range(1, NZ)]
     h_y = [
         [remote(part, part, hys.at[i, o - 1], hyr.at[i, o - 1], at_y(o)) for o in range(1, NY)]
         for i, part in enumerate(shares)
     ]
-    h_z.start()
-    for cp in h_y[0]:
+    nearest = (1, 7, 2, 6, 3, 5, 4)
+    for cp in [h_z[o - 1] for o in nearest] + h_y[0]:
         cp.start()
 
     for b in range(NX):
@@ -166,9 +165,10 @@
 
     lax.fori_loop(0, COLS // 512, turn, 0)
 
-    h_z.wait_recv()
-    for cp in h_y[1]:
-        cp.start()
+    for o in nearest:
+        h_z[o - 1].wait_recv()
+        for cp in h_y[o]:
+            cp.start()
     for o in (1, 3, 2):
         w_x[o - 1].wait_recv()
         w_c[o].start()
@@ -176,7 +176,7 @@
         cp.wait_send()
     for cp in t_x[0]:
         cp.start()
-    for cp in h_y[0] + h_y[1]:
+    for cp in sum(h_y, []):
         cp.wait_recv()
 
     mine = pl.ds(pl.multiple_of(x * CHIP, CHIP), CHIP)
@@ -443,7 +443,7 @@
             total = total + hgz[o, 16 * i : 16 * i + 16]
         hg_ref[16 * i : 16 * i + 16, :] = total[:, :WID].astype(BF16)
 
-    sent = h_x + [h_z, h_c] + w_c + s_x + s_y + s_z + c_x + c_y + c_z
+    sent = h_x + h_z + [h_c] + w_c + s_x + s_y + s_z + c_x + c_y + c_z
     for cp in sent + sum(h_y + t_x + g_a + g_f + g_c + h_to_y + h_to_z, []):
         cp.wait_send()
 
@@ -488,7 +488,7 @@
         vmem((NY, 8, BLK), F32),
         vmem((NZ, 8, BLK), F32),
     ]
-    counts = [(3,), (1,), (2, 3), (3,), (4,), (2, 3), (1,), (3,), (3,), (7,)]
+    counts = [(3,), (7,), (8, 3), (3,), (4,), (2, 3), (1,), (3,), (3,), (7,)]
     counts += [(8, 2), (8, 2), (8, 4), (8, 2), (2, 7), (3,), (3,), (7,)]
     sems = [dma((6,))]
     for n in counts:

time: 136 us -> 133 us (0.978)
  Pallas kernels: 136 us -> 132 us
    pallas_call x1, Pallas kernels: 133 us -> 129 us  [local(): pl.pallas_call(kernel, name='distill', out_shape=(vmem((1, BLK), F32), vm...]
where the time goes in v5:
time: 133 us; the launch traced here: 132 us
  Pallas kernels  132 us (99%)
    pallas_call x1, Pallas kernels, local(): pl.pallas_call(kernel, name='distill', out_shape=(vmem((1, BLK), F32), vm...  129 us

profile of v5, /device:TPU:24, one launch (start us, length us, event | category | flops | bytes accessed | tf_op | source)
XLA Modules:
  0.0 132.4 jit_solution(4288119327376522695)
XLA Ops:
  0.6 129.3 %distill.1 = (f32[1,128]{1,0:T(1,128)S(1)}, bf16[32,448]{1,0:T(8,128)(2,1)S(1)}, bf16[448,4096]{1,0:T(8,128)(2,1)S(1)}) custom-call(bf16[128,3584]{1,0:T(8,128)(2,1)} %h_ref.1, bf16[448,4096]{1,0:T(8,128)(2,1)} %w_ref.1, f32[128,4096]{1,0:T(8,128)} %t_ref.1), custom_call_target="tpu_custom_call" | custom-call | tf_op jit(solution)/shard_map/distill/pallas_call | solution.py:496
  129.9 2.5 %put.1 = (f32[128]{0:T(128)}, bf16[32,448]{1,0:T(8,128)(2,1)}, bf16[448,4096]{1,0:T(8,128)(2,1)}) custom-call(f32[1,128]{1,0:T(1,128)S(1)} %get-tuple-element.6.div_in, bf16[32,448]{1,0:T(8,128)(2,1)S(1)} %get-tuple-element.7.hg_in, bf16[448,4096]{1,0:T(8,128)(2,1)S(1)} %get-tuple-element.8.dw_in), custom_call_target="tpu_custom_call" | custom-call | tf_op jit(solution)/shard_map/put/pallas_call | solution.py:507

commit v6 on v5

--- a/solution.py
+++ b/solution.py
@@ -26,9 +26,9 @@
 BEFORE = (None, 0, None, 1, 2, 3, 4, 6)
 LAST = (5, 7)
 FIRST = tuple(128 * s for s in range(8))
+OFFERS = {0: 3, 2: 4, 3: 5, 4: 6, 6: 7}
 EARLY = 112
 WIDE = 512
-OFFERS = {0: 3, 2: 4, 3: 5, 4: 6, 6: 7}
 
 
 def groups(value):
@@ -54,9 +54,8 @@
     div_ref, hg_ref, dw_ref,
     hc, wc, tc, student, town, wown, wt, hx, ht, gbuf, acc,
     hgp, hgy, hgz, sx, sy, sz, last, col, cross, cx, cy, cz,
-    lsem, hxs, hxr, hzs, hzr, hys, hyr, wxs, wxr, wcs, wcr, ts, tr, hcs, hcr,
-    sxs, sxr, sys_, syr, szs, szr, gas, gar, gfs, gfr, gcs, gcr,
-    hgys, hgyr, hgzs, hgzr, cxs, cxr, cys, cyr, czs, czr,
+    lsem, own_s, own_r, two_s, two_r, wcs, wcr, ts, tr, hcs, hcr, sxs, sxr,
+    gfs, gfr, hgys, hgyr, hgzs, hgzr, cxs, cxr, cys, cyr, czs, czr,
 ):
     dp, v = lax.axis_index("dp"), lax.axis_index("vocab")
     x, c = dp // 2, dp % 2
@@ -103,13 +102,13 @@
 
     h_x = [
         remote(
-            h_ref.at[thin[0], share], hc.at[x, thin[0], share], hxs.at[o - 1], hxr.at[o - 1], at_x(o)
+            h_ref.at[thin[0], share], hc.at[x, thin[0], share], own_s.at[o - 1], own_r.at[o - 1], at_x(o)
         )
         for o in range(1, NX)
     ]
     w_x = [
         remote(
-            w_ref.at[:, cols_of(lax.rem(x + o, NX))], wc.at[wrows(x, c)], wxs.at[o - 1], wxr.at[o - 1], at_x(o)
+            w_ref.at[:, cols_of(lax.rem(x + o, NX))], wc.at[wrows(x, c)], own_s.at[o + 2], own_r.at[o + 2], at_x(o)
         )
         for o in range(1, NX)
     ]
@@ -137,9 +136,9 @@
     for cp in h_x:
         cp.wait_recv()
     shares = [hc.at[:, rows, share] for rows in thin]
-    h_z = [remote(shares[0], shares[0], hzs.at[o - 1], hzr.at[o - 1], at_z(o)) for o in range(1, NZ)]
+    h_z = [remote(shares[0], shares[0], two_s.at[o - 1, 3], two_r.at[o - 1, 3], at_z(o)) for o in range(1, NZ)]
     h_y = [
-        [remote(part, part, hys.at[i, o - 1], hyr.at[i, o - 1], at_y(o)) for o in range(1, NY)]
+        [remote(part, part, two_s.at[i, o - 1], two_r.at[i, o - 1], at_y(o)) for o in range(1, NY)]
         for i, part in enumerate(shares)
     ]
     nearest = (1, 7, 2, 6, 3, 5, 4)
@@ -172,8 +171,6 @@
     for o in (1, 3, 2):
         w_x[o - 1].wait_recv()
         w_c[o].start()
-    for cp in w_x:
-        cp.wait_send()
     for cp in t_x[0]:
         cp.start()
     for cp in sum(h_y, []):
@@ -223,8 +220,8 @@
         return put
 
     s_x = [remote(sx.at[x], sx.at[x], sxs.at[o - 1], sxr.at[o - 1], at_x(o)) for o in range(1, NX)]
-    s_y = [remote(sy.at[y], sy.at[y], sys_.at[o - 1], syr.at[o - 1], at_y(o)) for o in range(1, NY)]
-    s_z = [remote(sz.at[z], sz.at[z], szs.at[o - 1], szr.at[o - 1], at_z(o)) for o in range(1, NZ)]
+    s_y = [remote(sy.at[y], sy.at[y], own_s.at[o + 5], own_r.at[o + 5], at_y(o)) for o in range(1, NY)]
+    s_z = [remote(sz.at[z], sz.at[z], own_s.at[o + 8], own_r.at[o + 8], at_z(o)) for o in range(1, NZ)]
     for cp in s_y:
         cp.start()
     for cp in s_y:
@@ -247,6 +244,10 @@
 
     reduce_stats(sx, NX, columns)
 
+    keep.wait()
+    h_c.wait_recv()
+    for cp in h_x + w_x + h_z + sum(h_y, []) + s_x + s_y + s_z:
+        cp.wait_send()
     own_t.wait()
     for cp in t_x[0] + t_x[1]:
         cp.wait_recv()
@@ -271,7 +272,7 @@
     g_a, g_f, g_c = [], [], []
     for s in range(len(STEPS)):
         own, low, high = piece(s, x, 0, 1), piece(s, left, 0, 2), piece(s, right, 1, 2)
-        g_a.append([remote(own, own, gas.at[s, i], gar.at[s, i], at_x(o)) for i, o in enumerate((1, 3))])
+        g_a.append([remote(own, own, own_s.at[2 * s + i], own_r.at[2 * s + i], at_x(o)) for i, o in enumerate((1, 3))])
         g_f.append(
             [
                 remote(low, low, gfs.at[s, 0], gfr.at[s, 0], at_x(1)),
@@ -279,7 +280,7 @@
             ]
         )
         blocks = [piece(s, q, 0, 1) for q in owners]
-        g_c.append([remote(q, q, gcs.at[s, o], gcr.at[s, o], other) for o, q in enumerate(blocks)])
+        g_c.append([remote(q, q, two_s.at[s, o], two_r.at[s, o], other) for o, q in enumerate(blocks)])
 
     def make(s):
         rows, count = rows_mine(s), STEPS[s][2]
@@ -320,8 +321,6 @@
         cx[x, b] = jnp.broadcast_to(row_sum(cross[b]), (8, BLK))
     offer(1)
 
-    keep.wait()
-    h_c.wait_recv()
     for s in range(len(STEPS)):
         if s == 4:
             offer(2)
@@ -432,7 +431,7 @@
     for cp in c_z:
         cp.wait_recv()
     crossed = fold([cz[i, 0:1, :] for i in range(NZ)], jnp.add)
-    div_ref[...] = crossed / last[x, 1:2, :] + last[x, 0:1, :]
+    div_ref[...] = (crossed / last[x, 1:2, :] + last[x, 0:1, :])[0]
 
     for i in range(2):
         for cp in h_to_z[i]:
@@ -443,19 +442,18 @@
             total = total + hgz[o, 16 * i : 16 * i + 16]
         hg_ref[16 * i : 16 * i + 16, :] = total[:, :WID].astype(BF16)
 
-    sent = h_x + h_z + [h_c] + w_c + s_x + s_y + s_z + c_x + c_y + c_z
-    for cp in sent + sum(h_y + t_x + g_a + g_f + g_c + h_to_y + h_to_z, []):
+    sent = [h_c] + w_c + c_x + c_y + c_z
+    for cp in sent + sum(t_x + g_a + g_f + g_c + h_to_y + h_to_z, []):
         cp.wait_send()
 
 
 def put(div_in, hg_in, dw_in, div_ref, hg_ref, dw_ref, sems):
-    rows = WID // 7
-    parts = [pl.ds(rows * i, rows) for i in range(7)]
-    copies = [pltpu.make_async_copy(dw_in.at[p], dw_ref.at[p], sems.at[i]) for i, p in enumerate(parts)]
+    rows = WID // 4
+    parts = [(dw_in.at[pl.ds(rows * i, rows)], dw_ref.at[pl.ds(rows * i, rows)]) for i in range(4)]
+    parts += [(div_in, div_ref), (hg_in, hg_ref)]
+    copies = [pltpu.make_async_copy(src, dst, sems.at[i]) for i, (src, dst) in enumerate(parts)]
     for cp in copies:
         cp.start()
-    div_ref[...] = div_in[0]
-    hg_ref[...] = hg_in[...]
     for cp in copies:
         cp.wait()
 
@@ -488,15 +486,14 @@
         vmem((NY, 8, BLK), F32),
         vmem((NZ, 8, BLK), F32),
     ]
-    counts = [(3,), (7,), (8, 3), (3,), (4,), (2, 3), (1,), (3,), (3,), (7,)]
-    counts += [(8, 2), (8, 2), (8, 4), (8, 2), (2, 7), (3,), (3,), (7,)]
+    counts = [(16,), (8, 4), (4,), (2, 3), (1,), (3,), (8, 2), (8, 2), (2, 7), (3,), (3,), (7,)]
     sems = [dma((6,))]
     for n in counts:
         sems += [dma(n), dma(n)]
     div, hg, dw = pl.pallas_call(
         kernel,
         name="distill",
-        out_shape=(vmem((1, BLK), F32), vmem((SUB, WID), BF16), vmem((WID, COLS), BF16)),
+        out_shape=(vmem((BLK,), F32), vmem((SUB, WID), BF16), vmem((WID, COLS), BF16)),
         in_specs=[pl.BlockSpec(memory_space=pl.ANY)] * 3,
         out_specs=[pl.BlockSpec(memory_space=vmem)] * 3,
         scratch_shapes=scratch + sems,
@@ -513,8 +510,8 @@
             jax.ShapeDtypeStruct((WID, COLS), BF16),
         ),
         in_specs=[pl.BlockSpec(memory_space=vmem)] * 3,
-        out_specs=[pl.BlockSpec(memory_space=vmem)] * 2 + [pl.BlockSpec(memory_space=pl.ANY)],
-        scratch_shapes=[dma((7,))],
+        out_specs=[pl.BlockSpec(memory_space=pl.ANY)] * 3,
+        scratch_shapes=[dma((6,))],
         compiler_params=pltpu.CompilerParams(vmem_limit_bytes=2 * 1024 * 1024),
     )(div, hg, dw)
     return div, hg, dw

time: 133 us -> 131 us (0.985)
  Pallas kernels: 132 us -> 130 us
where the time goes in v6:
time: 131 us
  Pallas kernels  130 us (99%)
    pallas_call x1, Pallas kernels, local(): pl.pallas_call(kernel, name='distill', out_shape=(vmem((BLK,), F32), vmem...  129 us

profile of v6, /device:TPU:24, one launch (start us, length us, event | category | flops | bytes accessed | tf_op | source)
XLA Modules:
  0.0 131.0 jit_solution(6579806316001180934)
XLA Ops:
  0.6 128.5 %distill.1 = (f32[128]{0:T(128)S(1)}, bf16[32,448]{1,0:T(8,128)(2,1)S(1)}, bf16[448,4096]{1,0:T(8,128)(2,1)S(1)}) custom-call(bf16[128,3584]{1,0:T(8,128)(2,1)} %h_ref.1, bf16[448,4096]{1,0:T(8,128)(2,1)} %w_ref.1, f32[128,4096]{1,0:T(8,128)} %t_ref.1), custom_call_target="tpu_custom_call" | custom-call | tf_op jit(solution)/shard_map/distill/pallas_call | solution.py:493
  129.2 1.9 %put.1 = (f32[128]{0:T(128)}, bf16[32,448]{1,0:T(8,128)(2,1)}, bf16[448,4096]{1,0:T(8,128)(2,1)}) custom-call(f32[128]{0:T(128)S(1)} %get-tuple-element.6.div_in, bf16[32,448]{1,0:T(8,128)(2,1)S(1)} %get-tuple-element.7.hg_in, bf16[448,4096]{1,0:T(8,128)(2,1)S(1)} %get-tuple-element.8.dw_in), custom_call_target="tpu_custom_call" | custom-call | tf_op jit(solution)/shard_map/put/pallas_call | solution.py:504

commit v7 on v6

--- a/solution.py
+++ b/solution.py
@@ -26,7 +26,7 @@
 BEFORE = (None, 0, None, 1, 2, 3, 4, 6)
 LAST = (5, 7)
 FIRST = tuple(128 * s for s in range(8))
-OFFERS = {0: 3, 2: 4, 3: 5, 4: 6, 6: 7}
+OFFERS = {0: 2, 1: 3, 2: 4, 3: 5, 4: 6, 6: 7}
 EARLY = 112
 WIDE = 512
 
@@ -322,8 +322,6 @@
     offer(1)
 
     for s in range(len(STEPS)):
-        if s == 4:
-            offer(2)
         count = STEPS[s][2]
         block = jnp.concatenate([hx[j, b, rows_at(s, j), :] for j in range(2) for b in range(NX)], axis=0)
         block = pltpu.roll(block.astype(F32), lax.rem(c * WID, CHIP), 1)[:, :512]
@@ -406,7 +404,6 @@
     product(2)
     far_in(3)
     product(3)
-    head_product(0, 0, 2)
     far_in(4)
     near(5)
     near(6)
@@ -417,15 +414,13 @@
         cp.start()
     product(4)
     far_in(5)
-    head_product(0, 2, 4)
     product(5)
     far_in(6)
     near(7)
     product(6)
-    head_product(0, 4, 6)
     far_in(7)
     product(7)
-    head_product(0, 6, 8)
+    head_product(0, 0, 8)
     head_product(1, 0, 8)
 
     for cp in c_z:

time: 131 us -> 130 us (level)
  Pallas kernels: 130 us -> 128 us
    pallas_call x1, Pallas kernels: 129 us -> 127 us  [local(): pl.pallas_call(kernel, name='distill', out_shape=(vmem((BLK,), F32), vmem...]
where the time goes in v7:
time: 130 us; the launch traced here: 129 us
  Pallas kernels  128 us (98%)
    pallas_call x1, Pallas kernels, local(): pl.pallas_call(kernel, name='distill', out_shape=(vmem((BLK,), F32), vmem...  127 us

profile of v7, /device:TPU:24, one launch (start us, length us, event | category | flops | bytes accessed | tf_op | source)
XLA Modules:
  0.0 129.1 jit_solution(17938629899326172931)
XLA Ops:
  0.6 126.6 %distill.1 = (f32[128]{0:T(128)S(1)}, bf16[32,448]{1,0:T(8,128)(2,1)S(1)}, bf16[448,4096]{1,0:T(8,128)(2,1)S(1)}) custom-call(bf16[128,3584]{1,0:T(8,128)(2,1)} %h_ref.1, bf16[448,4096]{1,0:T(8,128)(2,1)} %w_ref.1, f32[128,4096]{1,0:T(8,128)} %t_ref.1), custom_call_target="tpu_custom_call" | custom-call | tf_op jit(solution)/shard_map/distill/pallas_call | solution.py:488
  127.2 1.9 %put.1 = (f32[128]{0:T(128)}, bf16[32,448]{1,0:T(8,128)(2,1)}, bf16[448,4096]{1,0:T(8,128)(2,1)}) custom-call(f32[128]{0:T(128)S(1)} %get-tuple-element.6.div_in, bf16[32,448]{1,0:T(8,128)(2,1)S(1)} %get-tuple-element.7.hg_in, bf16[448,4096]{1,0:T(8,128)(2,1)S(1)} %get-tuple-element.8.dw_in), custom_call_target="tpu_custom_call" | custom-call | tf_op jit(solution)/shard_map/put/pallas_call | solution.py:499
